TPU v7x, 256 devices: a whole 4x4x8 slice. The times are simulated.
256 devices in a mesh: row: 16 (over z, core), col: 16 (over y, x).
Axes of the slice: x: 4, y: 4, z: 8, core: 2. Of those that a mesh axis runs over, the one named last changes fastest.
Arguments:
- density: float32 [4096, 4096], P('row', 'col'), as said below
- pattern: int32 [32, 32], P('row', 'col'), may hold values from 0 to 1, as said below
Outputs:
- purified: float32 [4096, 4096], P('row', 'col')
Inputs may be any that keep to these rules, and one draw needn't show every extreme that they name: pattern is symmetric, with ones on the block diagonal. density is exactly symmetric and zero in every block where pattern is 0.
All inputs are finite; a program needn't handle non-finite values.
Results may differ from a plain program's by a relative error of at most 0.00016.
Values sent between devices are 32-bit elements; how exact they have to be, the bound alone decides.
A program may use at most 64 MiB of HBM per device.

v0:
```python
import jax
import jax.numpy as jnp
from jax import lax
from jax.sharding import PartitionSpec as P

BLOCK = 128
STEPS = 2


def expand_mask(pattern):
    widened = pattern.astype(jnp.float32)[:, None, :, None]
    shaped = jnp.broadcast_to(widened, (pattern.shape[0], BLOCK, pattern.shape[1], BLOCK))
    return shaped.reshape(pattern.shape[0] * BLOCK, pattern.shape[1] * BLOCK)


def local(density, pattern):
    block_mask = expand_mask(pattern)
    current = density
    for step in range(STEPS):
        column_block = lax.all_gather(current, "row", axis=0, tiled=True)

        def accumulate(piece):
            return jnp.dot(
                piece,
                column_block,
                precision=lax.Precision.HIGHEST,
                preferred_element_type=jnp.float32,
            )

        square = block_mask * accumulate(lax.all_gather(current, "col", axis=1, tiled=True))
        cubed = block_mask * accumulate(lax.all_gather(square, "col", axis=1, tiled=True))
        current = 3.0 * square - 2.0 * cubed
    return current


def solution(mesh):
    placed = (P("row", "col"), P("row", "col"))
    return jax.shard_map(
        local, mesh=mesh, in_specs=placed, out_specs=P("row", "col"), check_vma=False
    )
```

profile of v0, /device:TPU:1, one launch (start us, length us, event | category | flops | bytes accessed | tf_op | source)
XLA Modules:
  0.0 384.9 jit_solution(11668317890021914066)
XLA Ops:
  6.5 0.0 all-gather.7.cloned.1.call-start
  6.5 0.7 all-gather.7.cloned.1.call-update
  7.3 0.0 all-gather.9.cloned.1.call-start
  7.3 0.7 all-gather.9.cloned.1.call-update
  8.0 0.0 all-gather.11.cloned.1.call-start
  8.1 0.7 convert_element_type.3
  8.7 66.6 %all-gather.7.cloned.1.call-done = f32[256,4096]{1,0:T(8,128)} async-done(((f32[256,256]{1,0:T(8,128)}), f32[256,4096]{1,0:T(8,128)}) %all-gather.7.cloned.1.call-update) | async-done | bytes 4194320 | tf_op jit(solution)/shard_map/all_gather | solution.py:30
  75.3 44.7 %all-gather.9.cloned.1.call-done = f32[4096,256]{1,0:T(8,128)} async-done(((f32[256,256]{1,0:T(8,128)}), f32[4096,256]{1,0:T(8,128)}) %all-gather.9.cloned.1.call-update) | async-done | bytes 4194320 | tf_op jit(solution)/shard_map/all_gather | solution.py:20
  120.0 0.1 broadcast_in_dim.2
  120.1 7.8 %convolution_multiply_fusion.3 = f32[256,256]{1,0:T(8,128)} fusion(f32[256,4096]{1,0:T(8,128)} %all-gather.7.cloned.1.call-done, f32[4096,256]{1,0:T(8,128)} %all-gather.9.cloned.1.call-done, f32[32,8,2,128]{3,2,1,0:T(2,128)S(1)} %bitcast.15), kind=kOutput, calls=%fused_computation.5 | convolution fusion | flops 3221291008 | bytes 8912896 | tf_op jit(solution)/shard_map/dot_general | solution.py:23
  127.9 0.0 all-gather.11.cloned.1.call-update
  127.9 0.0 all-gather.13.cloned.1.call-start
  128.0 60.0 %all-gather.11.cloned.1.call-done = f32[256,4096]{1,0:T(8,128)} async-done(((f32[256,256]{1,0:T(8,128)}), f32[256,4096]{1,0:T(8,128)}) %all-gather.11.cloned.1.call-update) | async-done | bytes 4194320 | tf_op jit(solution)/shard_map/all_gather | solution.py:31
  187.9 7.8 %fusion.2 = f32[256,256]{1,0:T(8,128)} fusion(f32[256,4096]{1,0:T(8,128)} %all-gather.11.cloned.1.call-done, f32[4096,256]{1,0:T(8,128)} %all-gather.9.cloned.1.call-done, f32[256,256]{1,0:T(8,128)} %convolution_multiply_fusion.3, f32[32,8,2,128]{3,2,1,0:T(2,128)S(1)} %bitcast.16), kind=kOutput, calls=%fused_computation.6 | convolution fusion | flops 3221487616 | bytes 9175040 | tf_op jit(solution)/shard_map/dot_general | solution.py:23
  195.7 0.0 all-gather.13.cloned.1.call-update
  195.7 0.0 all-gather.15.cloned.1.call-start
  195.8 0.5 all-gather.15.cloned.1.call-update
  196.3 0.2 all-gather.17.cloned.1.call-start
  196.6 61.4 %all-gather.13.cloned.1.call-done = f32[256,4096]{1,0:T(8,128)} async-done(((f32[256,256]{1,0:T(8,128)}), f32[256,4096]{1,0:T(8,128)}) %all-gather.13.cloned.1.call-update) | async-done | bytes 4194320 | tf_op jit(solution)/shard_map/all_gather | solution.py:30
  257.9 44.6 %all-gather.15.cloned.1.call-done = f32[4096,256]{1,0:T(8,128)} async-done(((f32[256,256]{1,0:T(8,128)}), f32[4096,256]{1,0:T(8,128)}) %all-gather.15.cloned.1.call-update) | async-done | bytes 4194320 | tf_op jit(solution)/shard_map/all_gather | solution.py:20
  302.5 7.8 %convolution_multiply_fusion.1 = f32[256,256]{1,0:T(8,128)} fusion(f32[256,4096]{1,0:T(8,128)} %all-gather.13.cloned.1.call-done, f32[4096,256]{1,0:T(8,128)} %all-gather.15.cloned.1.call-done, f32[32,8,2,128]{3,2,1,0:T(2,128)S(1)} %bitcast.17), kind=kOutput, calls=%fused_computation.2 | convolution fusion | flops 3221291008 | bytes 8912896 | tf_op jit(solution)/shard_map/dot_general | solution.py:23
  310.2 0.0 all-gather.17.cloned.1.call-update
  310.3 60.0 %all-gather.17.cloned.1.call-done = f32[256,4096]{1,0:T(8,128)} async-done(((f32[256,256]{1,0:T(8,128)}), f32[256,4096]{1,0:T(8,128)}) %all-gather.17.cloned.1.call-update) | async-done | bytes 4194320 | tf_op jit(solution)/shard_map/all_gather | solution.py:31
  370.3 7.8 %fusion.3 = f32[256,256]{1,0:T(8,128)} fusion(f32[256,4096]{1,0:T(8,128)} %all-gather.17.cloned.1.call-done, f32[4096,256]{1,0:T(8,128)} %all-gather.15.cloned.1.call-done, f32[256,256]{1,0:T(8,128)} %convolution_multiply_fusion.1, f32[32,8,2,128]{3,2,1,0:T(2,128)S(1)} %bitcast.18), kind=kOutput, calls=%fused_computation.7 | convolution fusion | flops 3221487616 | bytes 9175040 | tf_op jit(solution)/shard_map/dot_general | solution.py:23
Async XLA Ops:
  6.5 68.8 %all-gather.7.cloned.1.call-start = ((), (), s32[]{:S(2)}) async-start(), calls=%async_computation | async-start | bytes 4456448 | tf_op jit(solution)/shard_map/all_gather | solution.py:30
  7.3 112.7 %all-gather.9.cloned.1.call-start = ((), (), s32[]{:S(2)}) async-start(), calls=%async_computation.1 | async-start | bytes 4456448 | tf_op jit(solution)/shard_map/all_gather | solution.py:20
  8.0 179.9 %all-gather.11.cloned.1.call-start = ((), (), s32[]{:S(2)}) async-start(), calls=%async_computation.2 | async-start | bytes 4456448 | tf_op jit(solution)/shard_map/all_gather | solution.py:31
  127.9 130.0 %all-gather.13.cloned.1.call-start = ((), (), s32[]{:S(2)}) async-start(), calls=%async_computation.3 | async-start | bytes 4456448 | tf_op jit(solution)/shard_map/all_gather | solution.py:30
  195.7 106.7 %all-gather.15.cloned.1.call-start = ((), (), s32[]{:S(2)}) async-start(), calls=%async_computation.4 | async-start | bytes 4456448 | tf_op jit(solution)/shard_map/all_gather | solution.py:20
  196.3 173.9 %all-gather.17.cloned.1.call-start = ((), (), s32[]{:S(2)}) async-start(), calls=%async_computation.5 | async-start | bytes 4456448 | tf_op jit(solution)/shard_map/all_gather | solution.py:31
Sparse Core Ops, SparseCore 0:
  9.8 65.4 all-gather.6
  77.1 42.8 all-gather.8
  128.1 59.8 all-gather.10
  195.9 62.0 all-gather.12
  259.6 42.8 all-gather.14
  310.4 59.8 all-gather.16
where the time goes:
time: 385 us
  waiting for transfers between devices  339 us (88%)
  matrix products  31.1 us (8%)
  between operations  13.5 us (4%)
    all_gather x2, waiting for transfers between devices, local(): lax.all_gather(current, 'col', axis=1, tiled=True)  128 us
    all_gather x2, waiting for transfers between devices, local(): lax.all_gather(square, 'col', axis=1, tiled=True)  120 us
    all_gather x2, waiting for transfers between devices, local(): column_block = lax.all_gather(current, 'row', axis=0, tiled=True)  89.3 us
    dot_general x4, matrix products, accumulate(): jnp.dot(piece, column_block, precision=lax.Precision.HIGHEST, preferred_e...  31.1 us
  transfers between devices with their start and end apart: 6, of which 6 were waited for; matrix products, arithmetic and copies ran while one was open for 0% of the time, Pallas kernels for 0%

commit v1 on v0

v1 whole, which is shorter than its diff:
```python
import heapq

import jax
import jax.numpy as jnp
from jax import lax
from jax.experimental import pallas as pl
from jax.experimental.pallas import tpu as pltpu
from jax.sharding import PartitionSpec as P

BLOCK = 128
STEPS = 2
NX, NY, NZ = 4, 4, 8
MESH = pl.DeviceIdType.MESH
f32, bf16 = jnp.float32, jnp.bfloat16
OFFSETS = [(dx, dy) for dx in (0, 1, -1, 2) for dy in (0, 1, -1, 2)]
RING = (0, 1, -1, 2, -2, 3, -3, 4)

ROWS64, HOP, PRODUCT, SMALL = 1.4, 1.0, 0.15, 0.05


def row_tile(p, h, plan, a, b):
    if (a, b) == (0, 0):
        return []
    parts = ("q0", "q1") if b == 2 or (b == 0 and a == 2) else ("h",)
    return [("row", p, h, plan, a, b, part) for part in parts]


def col_tile(s, h, dz, other):
    if other:
        return [("col", s, h, dz, "s")]
    if dz == 0:
        return []
    return [("col", s, h, dz, part) for part in (("q0", "q1") if dz == 4 else ("h",))]


def make_jobs():
    jobs = {}

    def link(plan, axis, sign):
        return ("x" if (axis == 0) == (plan == 0) else "y", sign)

    def own_row(p, h):
        pushes = []
        for axis in (0, 1):
            for plan in (0, 1):
                for sign in (1, -1):
                    a, b = (sign, 0) if axis == 0 else (0, sign)
                    pushes.append((link(plan, axis, sign), 1.0, ("row", p, h, plan, a, b, "h")))
        return pushes

    def own_col(s, h):
        return [(("z", sign), 2.0, ("col", s, h, sign, "h")) for sign in (1, -1)] + [
            (("core", 0), 0.3, ("col", s, h, 0, "s"))]

    def start(p, h):
        return ("start",) if p == 0 else ("final", p - 1, h)

    jobs[("start",)] = (0, SMALL, [], own_row(0, 0) + own_col(0, 0) + own_col(0, 1) + own_row(0, 1))
    for p in range(2 * STEPS):
        s = p // 2
        for h in (0, 1):
            for plan in (0, 1):
                for sign in (1, -1):
                    part = "q0" if sign == 1 else "q1"
                    for a in (0, 1, -1, 2):
                        pushes = [(link(plan, 1, sign), 0.5, ("row", p, h, plan, a, 2, part))]
                        jobs[("pass", p, h, plan, a, sign)] = (0, SMALL, row_tile(p, h, plan, a, sign), pushes)
                    pushes = [(link(plan, 0, sign), 0.5, ("row", p, h, plan, 2, 0, part))]
                    pushes += [(link(plan, 1, turn), 1.0, ("row", p, h, plan, sign, turn, "h")) for turn in (1, -1)]
                    jobs[("turn", p, h, plan, sign)] = (0, 3 * SMALL, row_tile(p, h, plan, sign, 0), pushes)
                pushes = [(link(plan, 1, turn), 1.0, ("row", p, h, plan, 2, turn, "h")) for turn in (1, -1)]
                jobs[("turn", p, h, plan, 2)] = (0, 2 * SMALL, row_tile(p, h, plan, 2, 0), pushes)
            if p % 2 == 0:
                for dz in RING:
                    pushes = []
                    if dz:
                        sign = 1 if dz > 0 else -1
                        if abs(dz) < 3:
                            pushes.append((("z", sign), 2.0, ("col", s, h, dz + sign, "h")))
                        elif dz != 4:
                            pushes.append((("z", sign), 1.0, ("col", s, h, 4, "q0" if sign == 1 else "q1")))
                        pushes.append((("core", 0), 0.3, ("col", s, h, dz, "s")))
                        jobs[("ring", s, h, dz)] = (0, 2 * SMALL, col_tile(s, h, dz, False), pushes)
                    before = [("ring", s, h, dz)] if dz else [start(p, h)]
                    jobs[("split", s, h, dz, False)] = (2, SMALL, before, [])
                    jobs[("split", s, h, dz, True)] = (2, SMALL, col_tile(s, h, dz, True), [])
            by_col = p == 0 and h == 0
            pieces = {o: row_tile(p, h, 0, *o) + row_tile(p, h, 1, *o[::-1]) for o in OFFSETS}
            if by_col:
                need = [piece for o in OFFSETS for piece in pieces[o]]
                keys = [(dz, other) for dz in RING for other in (False, True)]
                for key in keys:
                    jobs[("mac", p, h) + key] = (
                        4, PRODUCT, need + [("split", s, half, *key) for half in (0, 1)], [])
            else:
                keys = OFFSETS
                need = [("split", s, half, dz, other) for half in (0, 1) for dz in RING for other in (False, True)]
                for key in keys:
                    needs = pieces[key] + [start(p, h)] + (need if p % 2 == 0 else [])
                    jobs[("mac", p, h) + key] = (4 + p, PRODUCT, needs, [])
            pushes = []
            if p < 2 * STEPS - 1:
                pushes = own_row(p + 1, h) + (own_col(s + 1, h) if p % 2 else [])
            jobs[("final", p, h)] = (1, 2 * SMALL, [("mac", p, h) + key for key in keys], pushes)
    return jobs


def make_order(jobs):
    ready_at, missing, users = {}, {}, {}
    for name, (_, _, needs, _) in jobs.items():
        missing[name] = len(set(needs))
        ready_at[name] = 0.0
        for need in set(needs):
            users.setdefault(need, []).append(name)
    waiting, ready, free = [], [], {}
    rank = {name: n for n, name in enumerate(jobs)}

    def done(thing, when):
        for user in users.get(thing, ()):
            missing[user] -= 1
            ready_at[user] = max(ready_at[user], when)
            if missing[user] == 0:
                heapq.heappush(waiting, (ready_at[user], rank[user], user))

    for name in jobs:
        if missing[name] == 0:
            heapq.heappush(waiting, (0.0, rank[name], name))
    now, order = 0.0, []
    while waiting or ready:
        if not ready and waiting[0][0] > now:
            now = waiting[0][0]
        while waiting and waiting[0][0] <= now:
            when, number, name = heapq.heappop(waiting)
            heapq.heappush(ready, (jobs[name][0], when, number, name))
        name = heapq.heappop(ready)[-1]
        _, cost, _, pushes = jobs[name]
        now += cost
        order.append(name)
        for where, amount, piece in pushes:
            rate = 1.0 if where[0] == "core" else ROWS64
            free[where] = max(free.get(where, 0.0), now) + amount * rate
            done(piece, free[where] + HOP)
        done(name, now)
    return order, now


JOBS = make_jobs()
ORDER, MODEL_TIME = make_order(JOBS)
PIECES = [piece for name in JOBS for _, _, piece in JOBS[name][3]]
ROW = {name: n for n, name in enumerate(piece for piece in PIECES if piece[0] == "row")}
COL = {name: n for n, name in enumerate(piece for piece in PIECES if piece[0] == "col")}


def split(value):
    high = value.astype(bf16)
    return high, (value - high.astype(f32)).astype(bf16)


def kernel(pattern_in, density, out, rows, cols, col_hi, col_lo, acc, pattern,
           row_send, row_recv, col_send, col_recv, local_sem):
    size = density.shape[0]
    half, quarter, eighth = size // 2, size // 4, size // 8
    r, c = lax.axis_index("row"), lax.axis_index("col")
    z, core = r // 2, r % 2
    y, x = c // NX, c % NX

    def device(dx=0, dy=0, dz=0):
        return (((z + dz + NZ) % NZ) * 2 + core, ((y + dy + NY) % NY) * NX + (x + dx + NX) % NX)

    sibling = (z * 2 + 1 - core, c)

    def k_row(dx, dy):
        return ((y - dy + NY) % NY) * NX + (x - dx + NX) % NX

    def k_col(dz, other):
        return ((z - dz + NZ) % NZ) * 2 + (1 - core if other else core)

    fetch = [
        pltpu.make_async_copy(density, rows.at[0, c], local_sem.at[0]),
        pltpu.make_async_copy(density, cols.at[0, r], local_sem.at[1]),
        pltpu.make_async_copy(pattern_in, pattern, local_sem.at[2]),
    ]
    for copy in fetch:
        copy.start()

    peers = [device(dx=1), device(dx=-1), device(dy=1), device(dy=-1), device(dz=1), device(dz=-1), sibling]
    barrier = pltpu.get_barrier_semaphore()
    for peer in peers:
        pl.semaphore_signal(barrier, inc=1, device_id=peer, device_id_type=MESH)
    pl.semaphore_wait(barrier, len(peers))
    for copy in fetch:
        copy.wait()

    mask = [[pattern[a, b].astype(f32) for b in range(2)] for a in range(2)]

    def masked(value, h):
        return jnp.concatenate([value[:, :BLOCK] * mask[h][0], value[:, BLOCK:] * mask[h][1]], axis=1)

    def copy_of(piece, target):
        if piece[0] == "row":
            _, p, h, plan, a, b, part = piece
            dx, dy = (a, b) if plan == 0 else (b, a)
            low = h * half + plan * quarter + (eighth if part == "q1" else 0)
            return rows, p, low, quarter if part == "h" else eighth, row_send.at[p], row_recv.at[ROW[piece]], (dx, dy)
        _, s, h, dz, part = piece
        low = h * half + (quarter if part == "q1" else 0)
        return (cols, s, low, quarter if part in ("q0", "q1") else half, col_send.at[s], col_recv.at[COL[piece]], dz)

    def push(where, piece):
        buffer, index, low, count, send, recv, offset = copy_of(piece, None)
        axis, sign = where
        if piece[0] == "row":
            dx, dy = offset
            held = k_row(dx - sign, dy) if axis == "x" else k_row(dx, dy - sign)
        else:
            held = k_col(offset if axis == "core" else offset - sign, False)
        target = sibling if axis == "core" else device(**{"d" + axis: sign})
        part = buffer.at[index, held, pl.ds(low, count)]
        pltpu.make_async_remote_copy(
            src_ref=part, dst_ref=part, send_sem=send, recv_sem=recv,
            device_id=target, device_id_type=MESH).start()

    def wait(piece):
        buffer, index, low, count, send, recv, offset = copy_of(piece, None)
        if piece[0] == "row":
            held = k_row(*offset)
        else:
            held = k_col(offset, piece[-1] == "s")
        part = buffer.at[index, held, pl.ds(low, count)]
        pltpu.make_async_remote_copy(
            src_ref=part, dst_ref=part, send_sem=send, recv_sem=recv,
            device_id=sibling, device_id_type=MESH).wait_recv()

    waited, begun = set(), set()

    def run(name):
        _, _, needs, pushes = JOBS[name]
        for need in needs:
            if need[0] in ("row", "col") and need not in waited:
                waited.add(need)
                wait(need)
        kind = name[0]
        if kind == "split":
            _, s, h, dz, other = name
            k = k_col(dz, other)
            high, low = split(cols[s, k, pl.ds(h * half, half), :])
            col_hi[s, k, pl.ds(h * half, half), :] = high
            col_lo[s, k, pl.ds(h * half, half), :] = low
        elif kind == "mac":
            _, p, h = name[:3]
            by_col = isinstance(name[4], bool)
            k = k_col(*name[3:]) if by_col else k_row(*name[3:])
            high_a, low_a = split(rows[p, k, pl.ds(h * half, half), :])
            high_b, low_b = col_hi[p // 2, k], col_lo[p // 2, k]
            term = (jnp.dot(high_a, high_b, preferred_element_type=f32)
                    + jnp.dot(high_a, low_b, preferred_element_type=f32)
                    + jnp.dot(low_a, high_b, preferred_element_type=f32))
            if (p, h) in begun:
                acc[p, pl.ds(h * half, half), :] += term
            else:
                begun.add((p, h))
                acc[p, pl.ds(h * half, half), :] = term
        elif kind == "final":
            _, p, h = name
            here = pl.ds(h * half, half)
            value = masked(acc[p, here, :], h)
            if p % 2:
                value = 3.0 * rows[p, c, here, :] - 2.0 * value
            if p == 2 * STEPS - 1:
                out[here, :] = value
            else:
                rows[p + 1, c, here, :] = value
                if p % 2:
                    cols[p // 2 + 1, r, here, :] = value
        for where, _, piece in pushes:
            push(where, piece)

    for name in ORDER:
        run(name)

    for p in range(2 * STEPS):
        whole = rows.at[p, pl.ds(0, 15)]
        pltpu.make_async_copy(whole, whole, row_send.at[p]).wait()
    for s in range(STEPS):
        whole = cols.at[s, pl.ds(0, 15)]
        pltpu.make_async_copy(whole, whole, col_send.at[s]).wait()


def local(density, pattern):
    size = density.shape[0]
    tiles = NX * NY
    return pl.pallas_call(
        kernel,
        out_shape=jax.ShapeDtypeStruct(density.shape, f32),
        in_specs=[pl.BlockSpec(memory_space=pl.ANY), pl.BlockSpec(memory_space=pl.ANY)],
        out_specs=pl.BlockSpec(memory_space=pltpu.VMEM),
        scratch_shapes=[
            pltpu.VMEM((2 * STEPS, tiles, size, size), f32),
            pltpu.VMEM((STEPS, tiles, size, size), f32),
            pltpu.VMEM((STEPS, tiles, size, size), bf16),
            pltpu.VMEM((STEPS, tiles, size, size), bf16),
            pltpu.VMEM((2 * STEPS, size, size), f32),
            pltpu.SMEM(pattern.shape, jnp.int32),
            pltpu.SemaphoreType.DMA((2 * STEPS,)),
            pltpu.SemaphoreType.DMA((len(ROW),)),
            pltpu.SemaphoreType.DMA((STEPS,)),
            pltpu.SemaphoreType.DMA((len(COL),)),
            pltpu.SemaphoreType.DMA((3,)),
        ],
        compiler_params=pltpu.CompilerParams(
            collective_id=0, has_side_effects=True, vmem_limit_bytes=56 * 1024 * 1024),
    )(pattern, density)


def solution(mesh):
    placed = P("row", "col")
    return jax.shard_map(local, mesh=mesh, in_specs=(placed, placed), out_specs=placed, check_vma=False)
```

time: 385 us -> 116 us (0.30)
  waiting for transfers between devices: 339 us -> 0 us
  Pallas kernels: 0 us -> 115 us
  matrix products: 31.1 us -> 0 us
  between operations: 13.5 us -> 0.01 us
    all_gather x6 -> x0, waiting for transfers between devices: 337 us -> none  [the longest x2 128 us: local(): lax.all_gather(current, 'col', axis=1, tiled=True)]
    pallas_call x0 -> x1, Pallas kernels: none -> 115 us  [local(): pl.pallas_call(kernel, out_shape=jax.ShapeDtypeStruct(density.shape, f32)...]
    dot_general x4 -> x0, matrix products: 31.1 us -> none  [accumulate(): jnp.dot(piece, column_block, precision=lax.Precision.HIGHEST, preferred_e...]
  transfers between devices with their start and end apart: 6 -> 0, of which waited for: 6 -> 0; matrix products, arithmetic and copies ran while one was open for 0% -> 0% of each run, Pallas kernels for 0% -> 0%
where the time goes in v1:
time: 116 us
  Pallas kernels  115 us (99%)
  local copies, waits for them, and re-layouts  1.67 us (1%)
    pallas_call x1, Pallas kernels, local(): pl.pallas_call(kernel, out_shape=jax.ShapeDtypeStruct(density.shape, f32)...  115 us

profile of v1, /device:TPU:1, one launch (start us, length us, event | category | flops | bytes accessed | tf_op | source)
XLA Modules:
  0.0 116.2 jit_solution(12196194556706357650)
XLA Ops:
  0.0 114.5 %shard_map.28 = f32[256,256]{1,0:T(8,128)} custom-call(s32[2,2]{1,0:T(2,128)} %pattern_in.1, f32[256,256]{1,0:T(8,128)} %density.1), custom_call_target="tpu_custom_call" | custom-call | tf_op jit(solution)/shard_map/pallas_call | solution.py:292
  114.6 1.7 %copy.4 = f32[256,256]{1,0:T(8,128)} copy(f32[256,256]{1,0:T(8,128)} %shard_map.28) | data formatting | bytes 524288

commit v2 on v1

--- a/solution.py
+++ b/solution.py
@@ -15,14 +15,25 @@
 OFFSETS = [(dx, dy) for dx in (0, 1, -1, 2) for dy in (0, 1, -1, 2)]
 RING = (0, 1, -1, 2, -2, 3, -3, 4)
 
-ROWS64, HOP, PRODUCT, SMALL = 1.4, 1.0, 0.15, 0.05
+GROUPS = {}
+BEGIN = [(plan, sign) for plan in (0, 1) for sign in (1, -1)]
+
+ROWS64, HOP, SMALL, DOT, DOT_TILE = 1.31, 2.1, 0.03, 0.15, 0.12
+NEAR_FIRST = [
+    [(0, 0), (1, 0), (-1, 0), (0, 1), (0, -1)],
+    [(2, 0), (0, 2), (1, 1), (1, -1), (-1, 1), (-1, -1)],
+    [(1, 2), (-1, 2), (2, 1), (2, -1)],
+    [(2, 2)],
+]
+COL_GROUPS = [[0], [1, -1], [2, -2], [3, -3], [4]]
+
+
+def far_sign(h, plan, a=0):
+    return 1 if (h + plan + (0, 1, 2, 1)[a]) % 2 == 0 else -1
 
 
 def row_tile(p, h, plan, a, b):
-    if (a, b) == (0, 0):
-        return []
-    parts = ("q0", "q1") if b == 2 or (b == 0 and a == 2) else ("h",)
-    return [("row", p, h, plan, a, b, part) for part in parts]
+    return [] if (a, b) == (0, 0) else [("row", p, h, plan, a, b, "h")]
 
 
 def col_tile(s, h, dz, other):
@@ -49,59 +60,69 @@
         return pushes
 
     def own_col(s, h):
-        return [(("z", sign), 2.0, ("col", s, h, sign, "h")) for sign in (1, -1)] + [
-            (("core", 0), 0.3, ("col", s, h, 0, "s"))]
+        pushes = []
+        for t in (2 * h, 2 * h + 1):
+            pushes += [(("z", sign), 1.0, ("col", s, t, sign, "h")) for sign in (1, -1)]
+        return pushes + [(("core", 0), 0.15, ("col", s, t, 0, "s")) for t in (2 * h, 2 * h + 1)]
 
     def start(p, h):
         return ("start",) if p == 0 else ("final", p - 1, h)
 
-    jobs[("start",)] = (0, SMALL, [], own_row(0, 0) + own_col(0, 0) + own_col(0, 1) + own_row(0, 1))
+    def add(name, priority, cost, needs, pushes=()):
+        jobs[name] = (priority, cost + SMALL * (len(pushes) + len(needs)), needs, list(pushes))
+
+    add(("start",), 0, SMALL, [], own_row(0, 0) + own_col(0, 0) + own_col(0, 1) + own_row(0, 1))
     for p in range(2 * STEPS):
         s = p // 2
         for h in (0, 1):
             for plan in (0, 1):
                 for sign in (1, -1):
-                    part = "q0" if sign == 1 else "q1"
                     for a in (0, 1, -1, 2):
-                        pushes = [(link(plan, 1, sign), 0.5, ("row", p, h, plan, a, 2, part))]
-                        jobs[("pass", p, h, plan, a, sign)] = (0, SMALL, row_tile(p, h, plan, a, sign), pushes)
-                    pushes = [(link(plan, 0, sign), 0.5, ("row", p, h, plan, 2, 0, part))]
+                        if sign == far_sign(h, plan, a):
+                            add(("pass", p, h, plan, a, sign), 0, 0, row_tile(p, h, plan, a, sign),
+                                [(link(plan, 1, sign), 1.0, ("row", p, h, plan, a, 2, "h"))])
+                    pushes = []
+                    if sign == far_sign(h, plan):
+                        pushes = [(link(plan, 0, sign), 1.0, ("row", p, h, plan, 2, 0, "h"))]
                     pushes += [(link(plan, 1, turn), 1.0, ("row", p, h, plan, sign, turn, "h")) for turn in (1, -1)]
-                    jobs[("turn", p, h, plan, sign)] = (0, 3 * SMALL, row_tile(p, h, plan, sign, 0), pushes)
+                    add(("turn", p, h, plan, sign), 0, 0, row_tile(p, h, plan, sign, 0), pushes)
                 pushes = [(link(plan, 1, turn), 1.0, ("row", p, h, plan, 2, turn, "h")) for turn in (1, -1)]
-                jobs[("turn", p, h, plan, 2)] = (0, 2 * SMALL, row_tile(p, h, plan, 2, 0), pushes)
+                add(("turn", p, h, plan, 2), 0, 0, row_tile(p, h, plan, 2, 0), pushes)
             if p % 2 == 0:
-                for dz in RING:
+                for t, dz in ((t, dz) for dz in RING for t in (2 * h, 2 * h + 1)):
                     pushes = []
                     if dz:
                         sign = 1 if dz > 0 else -1
                         if abs(dz) < 3:
-                            pushes.append((("z", sign), 2.0, ("col", s, h, dz + sign, "h")))
+                            pushes.append((("z", sign), 1.0, ("col", s, t, dz + sign, "h")))
                         elif dz != 4:
-                            pushes.append((("z", sign), 1.0, ("col", s, h, 4, "q0" if sign == 1 else "q1")))
-                        pushes.append((("core", 0), 0.3, ("col", s, h, dz, "s")))
-                        jobs[("ring", s, h, dz)] = (0, 2 * SMALL, col_tile(s, h, dz, False), pushes)
-                    before = [("ring", s, h, dz)] if dz else [start(p, h)]
-                    jobs[("split", s, h, dz, False)] = (2, SMALL, before, [])
-                    jobs[("split", s, h, dz, True)] = (2, SMALL, col_tile(s, h, dz, True), [])
-            by_col = p == 0 and h == 0
+                            pushes.append((("z", sign), 0.5, ("col", s, t, 4, "q0" if sign == 1 else "q1")))
+                        pushes.append((("core", 0), 0.15, ("col", s, t, dz, "s")))
+                        add(("ring", s, t, dz), 0, 0, col_tile(s, t, dz, False), pushes)
+                    before = [("ring", s, t, dz)] if dz else [start(p, h)]
+                    add(("split", s, t, dz, False), 2, SMALL, before)
+                    add(("split", s, t, dz, True), 2, SMALL, col_tile(s, t, dz, True))
             pieces = {o: row_tile(p, h, 0, *o) + row_tile(p, h, 1, *o[::-1]) for o in OFFSETS}
-            if by_col:
+            if p % 2 == 0 and h == 0:
                 need = [piece for o in OFFSETS for piece in pieces[o]]
-                keys = [(dz, other) for dz in RING for other in (False, True)]
-                for key in keys:
-                    jobs[("mac", p, h) + key] = (
-                        4, PRODUCT, need + [("split", s, half, *key) for half in (0, 1)], [])
+                groups = [[(dz, other) for dz in group for other in (False, True)] for group in COL_GROUPS]
+                needs = [need + [("split", s, t, *key) for t in range(4) for key in group] for group in groups]
             else:
-                keys = OFFSETS
-                need = [("split", s, half, dz, other) for half in (0, 1) for dz in RING for other in (False, True)]
-                for key in keys:
-                    needs = pieces[key] + [start(p, h)] + (need if p % 2 == 0 else [])
-                    jobs[("mac", p, h) + key] = (4 + p, PRODUCT, needs, [])
+                groups = NEAR_FIRST
+                need = [("split", s, t, dz, other) for t in range(4) for dz in RING for other in (False, True)]
+                needs = [[piece for key in group for piece in pieces[key]] + [start(p, h)] + (need if p % 2 == 0 else [])
+                         for group in groups]
+            for n, group in enumerate(groups):
+                jobs[("mac", p, h, n)] = (4 + p, DOT + DOT_TILE * len(group), needs[n], [])
+                GROUPS[p, h, n] = group
             pushes = []
             if p < 2 * STEPS - 1:
                 pushes = own_row(p + 1, h) + (own_col(s + 1, h) if p % 2 else [])
-            jobs[("final", p, h)] = (1, 2 * SMALL, [("mac", p, h) + key for key in keys], pushes)
+            if p % 2 == 0 and h:
+                add(("final", p, h), 1, 2 * SMALL, [("mac", p, h, n) for n in range(len(groups))])
+                add(("begin", p, h), 1, 0, [("final", p, h)] + [("turn", p + 1, 0, *key) for key in BEGIN], pushes)
+            else:
+                add(("final", p, h), 1, 2 * SMALL, [("mac", p, h, n) for n in range(len(groups))], pushes)
     return jobs
 
 
@@ -125,7 +146,7 @@
     for name in jobs:
         if missing[name] == 0:
             heapq.heappush(waiting, (0.0, rank[name], name))
-    now, order = 0.0, []
+    now, order, times = 0.0, [], {}
     while waiting or ready:
         if not ready and waiting[0][0] > now:
             now = waiting[0][0]
@@ -136,16 +157,17 @@
         _, cost, _, pushes = jobs[name]
         now += cost
         order.append(name)
+        times[name] = now
         for where, amount, piece in pushes:
             rate = 1.0 if where[0] == "core" else ROWS64
             free[where] = max(free.get(where, 0.0), now) + amount * rate
             done(piece, free[where] + HOP)
         done(name, now)
-    return order, now
+    return order, times
 
 
 JOBS = make_jobs()
-ORDER, MODEL_TIME = make_order(JOBS)
+ORDER, TIMES = make_order(JOBS)
 PIECES = [piece for name in JOBS for _, _, piece in JOBS[name][3]]
 ROW = {name: n for n, name in enumerate(piece for piece in PIECES if piece[0] == "row")}
 COL = {name: n for n, name in enumerate(piece for piece in PIECES if piece[0] == "col")}
@@ -200,11 +222,11 @@
         if piece[0] == "row":
             _, p, h, plan, a, b, part = piece
             dx, dy = (a, b) if plan == 0 else (b, a)
-            low = h * half + plan * quarter + (eighth if part == "q1" else 0)
-            return rows, p, low, quarter if part == "h" else eighth, row_send.at[p], row_recv.at[ROW[piece]], (dx, dy)
+            low = h * half + plan * quarter
+            return rows, p, low, quarter, row_send.at[p], row_recv.at[ROW[piece]], (dx, dy)
         _, s, h, dz, part = piece
-        low = h * half + (quarter if part == "q1" else 0)
-        return (cols, s, low, quarter if part in ("q0", "q1") else half, col_send.at[s], col_recv.at[COL[piece]], dz)
+        low = h * quarter + (eighth if part == "q1" else 0)
+        return (cols, s, low, eighth if part in ("q0", "q1") else quarter, col_send.at[s], col_recv.at[COL[piece]], dz)
 
     def push(where, piece):
         buffer, index, low, count, send, recv, offset = copy_of(piece, None)
@@ -243,23 +265,26 @@
         if kind == "split":
             _, s, h, dz, other = name
             k = k_col(dz, other)
-            high, low = split(cols[s, k, pl.ds(h * half, half), :])
-            col_hi[s, k, pl.ds(h * half, half), :] = high
-            col_lo[s, k, pl.ds(h * half, half), :] = low
+            here = pl.ds(h * quarter, quarter)
+            high, low = split(cols[s, k, here, :])
+            col_hi[s, k, here, :] = high
+            col_lo[s, k, here, :] = low
         elif kind == "mac":
             _, p, h = name[:3]
-            by_col = isinstance(name[4], bool)
-            k = k_col(*name[3:]) if by_col else k_row(*name[3:])
-            high_a, low_a = split(rows[p, k, pl.ds(h * half, half), :])
-            high_b, low_b = col_hi[p // 2, k], col_lo[p // 2, k]
-            term = (jnp.dot(high_a, high_b, preferred_element_type=f32)
-                    + jnp.dot(high_a, low_b, preferred_element_type=f32)
-                    + jnp.dot(low_a, high_b, preferred_element_type=f32))
+            here = pl.ds(h * half, half)
+            term = None
+            for key in GROUPS[name[1:]]:
+                k = k_col(*key) if isinstance(key[1], bool) else k_row(*key)
+                high_a, low_a = split(rows[p, k, here, :])
+                high_b, low_b = col_hi[p // 2, k], col_lo[p // 2, k]
+                for one, other in ((high_a, high_b), (high_a, low_b), (low_a, high_b)):
+                    dot = jnp.dot(one, other, preferred_element_type=f32)
+                    term = dot if term is None else term + dot
             if (p, h) in begun:
-                acc[p, pl.ds(h * half, half), :] += term
+                acc[p, here, :] += term
             else:
                 begun.add((p, h))
-                acc[p, pl.ds(h * half, half), :] = term
+                acc[p, here, :] = term
         elif kind == "final":
             _, p, h = name
             here = pl.ds(h * half, half)
@@ -292,7 +317,7 @@
     return pl.pallas_call(
         kernel,
         out_shape=jax.ShapeDtypeStruct(density.shape, f32),
-        in_specs=[pl.BlockSpec(memory_space=pl.ANY), pl.BlockSpec(memory_space=pl.ANY)],
+        in_specs=[pl.BlockSpec(memory_space=pltpu.HBM), pl.BlockSpec(memory_space=pltpu.HBM)],
         out_specs=pl.BlockSpec(memory_space=pltpu.VMEM),
         scratch_shapes=[
             pltpu.VMEM((2 * STEPS, tiles, size, size), f32),

time: 116 us -> 115 us (level)
  Pallas kernels: 115 us -> 113 us
    pallas_call x1, Pallas kernels: 115 us -> 113 us  [local(): pl.pallas_call(kernel, out_shape=jax.ShapeDtypeStruct(density.shape, f32)...]
where the time goes in v2:
time: 115 us
  Pallas kernels  113 us (98%)
  local copies, waits for them, and re-layouts  1.67 us (1%)
    pallas_call x1, Pallas kernels, local(): pl.pallas_call(kernel, out_shape=jax.ShapeDtypeStruct(density.shape, f32)...  113 us

profile of v2, /device:TPU:1, one launch (start us, length us, event | category | flops | bytes accessed | tf_op | source)
XLA Modules:
  0.0 114.8 jit_solution(17598192297061943153)
XLA Ops:
  0.0 113.1 %shard_map.28 = f32[256,256]{1,0:T(8,128)} custom-call(s32[2,2]{1,0:T(2,128)} %pattern_in.1, f32[256,256]{1,0:T(8,128)} %density.1), custom_call_target="tpu_custom_call" | custom-call | tf_op jit(solution)/shard_map/pallas_call | solution.py:317
  113.1 1.7 %copy.4 = f32[256,256]{1,0:T(8,128)} copy(f32[256,256]{1,0:T(8,128)} %shard_map.28) | data formatting | bytes 524288

commit v3 on v2

v3 whole, which is shorter than its diff:
```python
import heapq

import jax
import jax.numpy as jnp
from jax import lax
from jax.experimental import pallas as pl
from jax.experimental.pallas import tpu as pltpu
from jax.sharding import PartitionSpec as P

BLOCK = 128
STEPS = 2
NX, NY, NZ = 4, 4, 8
MESH = pl.DeviceIdType.MESH
f32, bf16 = jnp.float32, jnp.bfloat16
OFFSETS = [(dx, dy) for dx in (0, 1, -1, 2) for dy in (0, 1, -1, 2)]
RING = (0, 1, -1, 2, -2, 3, -3, 4)

GROUPS = {}
BEGIN_ROWS = [(0, 2), (1, 2)]
BEGIN_COLS = (1, -1)
BEGIN = [(plan, sign) for plan in (0, 1) for sign in (1, -1)]

ROWS64, HOP, SMALL, DOT, DOT_TILE = 1.31, 2.1, 0.03, 0.15, 0.12
NEAR_FIRST = [
    [(0, 0), (1, 0), (-1, 0), (0, 1), (0, -1)],
    [(2, 0), (0, 2), (1, 1), (1, -1), (-1, 1), (-1, -1)],
    [(1, 2), (-1, 2), (2, 1), (2, -1)],
    [(2, 2)],
]
COL_GROUPS = [[0], [1, -1], [2, -2], [3, -3], [4]]


HALVES = [(0, 128, 0, 256), (128, 128, 0, 256)]
SQUARE = [(0, 128, 0, 128), (0, 128, 128, 128), (128, 128, 0, 256)]
STREAMS = [HALVES, SQUARE, HALVES, SQUARE, HALVES]
COLUMNS = [(0, 128, 0, 128), (128, 128, 0, 128), (0, 128, 128, 128), (128, 128, 128, 128)]
COL_SIZE = 1.0


def far_sign(h, plan, a=0):
    return 1 if (h + plan + (0, 1, 2, 1)[a]) % 2 == 0 else -1


def row_tile(p, h, plan, a, b):
    return [] if (a, b) == (0, 0) else [("row", p, h, plan, a, b, "h")]


def col_tile(s, t, dz, other):
    if other:
        return [("col", s, t, dz, "s")]
    if dz == 0:
        return []
    return [("col", s, t, dz, part) for part in (("q0", "q1") if dz == 4 else ("h",))]


def make_jobs():
    jobs = {}

    def link(plan, axis, sign):
        return ("x" if (axis == 0) == (plan == 0) else "y", sign)

    def row_size(p, h):
        return STREAMS[p][h][1] * STREAMS[p][h][3] / (128 * 256)

    def own_row(p, h):
        pushes = []
        for axis in (0, 1):
            for plan in (0, 1):
                for sign in (1, -1):
                    a, b = (sign, 0) if axis == 0 else (0, sign)
                    pushes.append((link(plan, axis, sign), row_size(p, h), ("row", p, h, plan, a, b, "h")))
        return pushes

    def own_col(s, ts):
        pushes = []
        for t in ts:
            pushes += [(("z", sign), COL_SIZE, ("col", s, t, sign, "h")) for sign in (1, -1)]
        return pushes + [(("core", 0), 0.15, ("col", s, t, 0, "s")) for t in ts]

    def overlap(one, other):
        return all(one[i] < other[i] + other[i + 1] and other[i] < one[i] + one[i + 1] for i in (0, 2))

    def add(name, priority, cost, needs, pushes=()):
        jobs[name] = (priority, cost + SMALL * (len(pushes) + len(needs)), needs, list(pushes))

    add(("start",), 0, SMALL, [], own_row(0, 0) + own_col(0, (0, 1)))
    add(("begin", 0, 1), 0, 0, [("turn", 0, 0, *key) for key in BEGIN_ROWS], own_row(0, 1))
    add(("begin_col",), 0, 0, [("ring", 0, t, dz) for t in (0, 1) for dz in BEGIN_COLS], own_col(0, (2, 3)))
    for p in range(2 * STEPS):
        s = p // 2
        for h, stream in enumerate(STREAMS[p]):
            size = row_size(p, h)
            for plan in (0, 1):
                for sign in (1, -1):
                    for a in (0, 1, -1, 2):
                        if sign == far_sign(h, plan, a):
                            add(("pass", p, h, plan, a, sign), 0, 0, row_tile(p, h, plan, a, sign),
                                [(link(plan, 1, sign), size, ("row", p, h, plan, a, 2, "h"))])
                    pushes = []
                    if sign == far_sign(h, plan):
                        pushes = [(link(plan, 0, sign), size, ("row", p, h, plan, 2, 0, "h"))]
                    pushes += [(link(plan, 1, turn), size, ("row", p, h, plan, sign, turn, "h")) for turn in (1, -1)]
                    add(("turn", p, h, plan, sign), 0, 0, row_tile(p, h, plan, sign, 0), pushes)
                pushes = [(link(plan, 1, turn), size, ("row", p, h, plan, 2, turn, "h")) for turn in (1, -1)]
                add(("turn", p, h, plan, 2), 0, 0, row_tile(p, h, plan, 2, 0), pushes)
        if p % 2 == 0:
            for t, dz in ((t, dz) for dz in RING for t in range(4)):
                pushes = []
                if dz:
                    sign = 1 if dz > 0 else -1
                    if abs(dz) < 3:
                        pushes.append((("z", sign), COL_SIZE, ("col", s, t, dz + sign, "h")))
                    elif dz != 4:
                        pushes.append((("z", sign), COL_SIZE / 2, ("col", s, t, 4, "q0" if sign == 1 else "q1")))
                    pushes.append((("core", 0), 0.15, ("col", s, t, dz, "s")))
                    add(("ring", s, t, dz), 0, 0, col_tile(s, t, dz, False), pushes)
                before = [("ring", s, t, dz)] if dz else [("start",) if p == 0 else ("final", p - 1, t % 2)]
                add(("split", s, t, dz, False), 2, SMALL, before)
                add(("split", s, t, dz, True), 2, SMALL, col_tile(s, t, dz, True))
        for o, target in enumerate(STREAMS[p + 1]):
            rows_used = [h for h, stream in enumerate(STREAMS[p]) if overlap(stream, (target[0], target[1], 0, 256))]
            cols_used = [t for t, col in enumerate(COLUMNS) if overlap(col, (0, 256, target[2], target[3]))]
            pieces = {key: [piece for h in rows_used
                            for piece in row_tile(p, h, 0, *key) + row_tile(p, h, 1, *key[::-1])] for key in OFFSETS}
            starts = [("start",) if p == 0 else ("final", p - 1, h) for h in rows_used]
            if p % 2 == 0 and target[0] == 0:
                need = [piece for key in OFFSETS for piece in pieces[key]] + starts
                groups = [[(dz, other) for dz in group for other in (False, True)] for group in COL_GROUPS]
                needs = [need + [("split", s, t, *key) for t in cols_used for key in group] for group in groups]
            else:
                groups = NEAR_FIRST
                need = [("split", s, t, dz, other) for t in cols_used for dz in RING for other in (False, True)]
                needs = [[piece for key in group for piece in pieces[key]] + starts + (need if p % 2 == 0 else [])
                         for group in groups]
            for n, group in enumerate(groups):
                cost = DOT + DOT_TILE * len(group) * (0.6 if target[3] == 128 else 1)
                jobs[("mac", p, o, n)] = (4 + p, cost, needs[n], [])
                GROUPS[p, o, n] = group
            pushes = []
            if p < 2 * STEPS - 1:
                pushes = own_row(p + 1, o) + (own_col(s + 1, (o, 2 + o)) if p % 2 else [])
            macs = [("mac", p, o, n) for n in range(len(groups))]
            if p % 2 == 0 and o == 2:
                add(("final", p, o), 1, 2 * SMALL, macs)
                add(("begin", p, o), 1, 0, [("final", p, o)] + [("turn", p + 1, 1, *key) for key in BEGIN], pushes)
            else:
                add(("final", p, o), 1, 2 * SMALL, macs, pushes)
    return jobs


def make_order(jobs):
    ready_at, missing, users = {}, {}, {}
    for name, (_, _, needs, _) in jobs.items():
        missing[name] = len(set(needs))
        ready_at[name] = 0.0
        for need in set(needs):
            users.setdefault(need, []).append(name)
    waiting, ready, free = [], [], {}
    rank = {name: n for n, name in enumerate(jobs)}

    def done(thing, when):
        for user in users.get(thing, ()):
            missing[user] -= 1
            ready_at[user] = max(ready_at[user], when)
            if missing[user] == 0:
                heapq.heappush(waiting, (ready_at[user], rank[user], user))

    for name in jobs:
        if missing[name] == 0:
            heapq.heappush(waiting, (0.0, rank[name], name))
    now, order, times = 0.0, [], {}
    while waiting or ready:
        if not ready and waiting[0][0] > now:
            now = waiting[0][0]
        while waiting and waiting[0][0] <= now:
            when, number, name = heapq.heappop(waiting)
            heapq.heappush(ready, (jobs[name][0], when, number, name))
        name = heapq.heappop(ready)[-1]
        _, cost, _, pushes = jobs[name]
        now += cost
        order.append(name)
        times[name] = now
        for where, amount, piece in pushes:
            rate = 1.0 if where[0] == "core" else ROWS64
            free[where] = max(free.get(where, 0.0), now) + amount * rate
            done(piece, free[where] + HOP)
        done(name, now)
    return order, times


JOBS = make_jobs()
ORDER, TIMES = make_order(JOBS)
PIECES = [piece for name in JOBS for _, _, piece in JOBS[name][3]]
ROW = {name: n for n, name in enumerate(piece for piece in PIECES if piece[0] == "row")}
COL = {name: n for n, name in enumerate(piece for piece in PIECES if piece[0] == "col")}


def split(value):
    high = value.astype(bf16)
    return high, (value - high.astype(f32)).astype(bf16)


def kernel(pattern_in, density, out, rows, cols, col_hi, col_lo, acc, pattern,
           row_send, row_recv, col_send, col_recv, local_sem):
    size = density.shape[0]
    r, c = lax.axis_index("row"), lax.axis_index("col")
    z, core = r // 2, r % 2
    y, x = c // NX, c % NX

    def device(dx=0, dy=0, dz=0):
        return (((z + dz + NZ) % NZ) * 2 + core, ((y + dy + NY) % NY) * NX + (x + dx + NX) % NX)

    sibling = (z * 2 + 1 - core, c)

    def k_row(dx, dy):
        return ((y - dy + NY) % NY) * NX + (x - dx + NX) % NX

    def k_col(dz, other):
        return ((z - dz + NZ) % NZ) * 2 + (1 - core if other else core)

    fetch = [
        pltpu.make_async_copy(density, rows.at[0, c], local_sem.at[0]),
        pltpu.make_async_copy(density, cols.at[0, r], local_sem.at[1]),
        pltpu.make_async_copy(pattern_in, pattern, local_sem.at[2]),
    ]
    for copy in fetch:
        copy.start()

    peers = [device(dx=1), device(dx=-1), device(dy=1), device(dy=-1), device(dz=1), device(dz=-1), sibling]
    barrier = pltpu.get_barrier_semaphore()
    for peer in peers:
        pl.semaphore_signal(barrier, inc=1, device_id=peer, device_id_type=MESH)
    pl.semaphore_wait(barrier, len(peers))
    for copy in fetch:
        copy.wait()

    mask = [[pattern[a, b].astype(f32) for b in range(2)] for a in range(2)]

    def masked(value, low, lane):
        parts = [value[:, n:n + BLOCK] * mask[low // BLOCK][(lane + n) // BLOCK] for n in range(0, value.shape[1], BLOCK)]
        return jnp.concatenate(parts, axis=1)

    def copy_of(piece):
        if piece[0] == "row":
            _, p, h, plan, a, b, _ = piece
            low, count, lane, lanes = STREAMS[p][h]
            here = pl.ds(low + plan * (count // 2), count // 2), pl.ds(lane, lanes)
            return rows, p, here, row_send.at[p], row_recv.at[ROW[piece]], (a, b) if plan == 0 else (b, a)
        _, s, t, dz, part = piece
        low, count, lane, lanes = COLUMNS[t]
        if part in ("q0", "q1"):
            count //= 2
            low += count if part == "q1" else 0
        here = pl.ds(low, count), pl.ds(lane, lanes)
        return cols, s, here, col_send.at[s], col_recv.at[COL[piece]], dz

    def push(where, piece):
        buffer, index, here, send, recv, offset = copy_of(piece)
        axis, sign = where
        if piece[0] == "row":
            dx, dy = offset
            held = k_row(dx - sign, dy) if axis == "x" else k_row(dx, dy - sign)
        else:
            held = k_col(offset if axis == "core" else offset - sign, False)
        target = sibling if axis == "core" else device(**{"d" + axis: sign})
        part = buffer.at[index, held, *here]
        pltpu.make_async_remote_copy(
            src_ref=part, dst_ref=part, send_sem=send, recv_sem=recv,
            device_id=target, device_id_type=MESH).start()

    def wait(piece):
        buffer, index, here, send, recv, offset = copy_of(piece)
        if piece[0] == "row":
            held = k_row(*offset)
        else:
            held = k_col(offset, piece[-1] == "s")
        part = buffer.at[index, held, *here]
        pltpu.make_async_remote_copy(
            src_ref=part, dst_ref=part, send_sem=send, recv_sem=recv,
            device_id=sibling, device_id_type=MESH).wait_recv()

    waited, begun = set(), set()

    def run(name):
        _, _, needs, pushes = JOBS[name]
        for need in needs:
            if need[0] in ("row", "col") and need not in waited:
                waited.add(need)
                wait(need)
        kind = name[0]
        if kind == "split":
            _, s, t, dz, other = name
            k = k_col(dz, other)
            here = pl.ds(*COLUMNS[t][:2]), pl.ds(*COLUMNS[t][2:])
            high, low = split(cols[s, k, *here])
            col_hi[s, k, *here] = high
            col_lo[s, k, *here] = low
        elif kind == "mac":
            _, p, o = name[:3]
            low, count, lane, lanes = STREAMS[p + 1][o]
            here, wide = pl.ds(low, count), pl.ds(lane, lanes)
            term = None
            for key in GROUPS[name[1:]]:
                k = k_col(*key) if isinstance(key[1], bool) else k_row(*key)
                high_a, low_a = split(rows[p, k, here, :])
                high_b, low_b = col_hi[p // 2, k, :, wide], col_lo[p // 2, k, :, wide]
                for one, other in ((high_a, high_b), (high_a, low_b), (low_a, high_b)):
                    dot = jnp.dot(one, other, preferred_element_type=f32)
                    term = dot if term is None else term + dot
            if (p, o) in begun:
                acc[p, here, wide] += term
            else:
                begun.add((p, o))
                acc[p, here, wide] = term
        elif kind == "final":
            _, p, o = name
            low, count, lane, lanes = STREAMS[p + 1][o]
            here, wide = pl.ds(low, count), pl.ds(lane, lanes)
            value = masked(acc[p, here, wide], low, lane)
            if p % 2:
                value = 3.0 * rows[p, c, here, wide] - 2.0 * value
            if p == 2 * STEPS - 1:
                out[here, wide] = value
            else:
                rows[p + 1, c, here, wide] = value
                if p % 2:
                    cols[p // 2 + 1, r, here, wide] = value
        for where, _, piece in pushes:
            push(where, piece)

    for name in ORDER:
        run(name)

    for p in range(2 * STEPS):
        whole = rows.at[p, pl.ds(0, 15)]
        pltpu.make_async_copy(whole, whole, row_send.at[p]).wait()
    for s in range(STEPS):
        whole = cols.at[s, pl.ds(0, 15)]
        pltpu.make_async_copy(whole, whole, col_send.at[s]).wait()


def local(density, pattern):
    size = density.shape[0]
    tiles = NX * NY
    return pl.pallas_call(
        kernel,
        out_shape=jax.ShapeDtypeStruct(density.shape, f32),
        in_specs=[pl.BlockSpec(memory_space=pltpu.HBM), pl.BlockSpec(memory_space=pltpu.HBM)],
        out_specs=pl.BlockSpec(memory_space=pltpu.VMEM),
        scratch_shapes=[
            pltpu.VMEM((2 * STEPS, tiles, size, size), f32),
            pltpu.VMEM((STEPS, tiles, size, size), f32),
            pltpu.VMEM((STEPS, tiles, size, size), bf16),
            pltpu.VMEM((STEPS, tiles, size, size), bf16),
            pltpu.VMEM((2 * STEPS, size, size), f32),
            pltpu.SMEM(pattern.shape, jnp.int32),
            pltpu.SemaphoreType.DMA((2 * STEPS,)),
            pltpu.SemaphoreType.DMA((len(ROW),)),
            pltpu.SemaphoreType.DMA((STEPS,)),
            pltpu.SemaphoreType.DMA((len(COL),)),
            pltpu.SemaphoreType.DMA((3,)),
        ],
        compiler_params=pltpu.CompilerParams(
            collective_id=0, has_side_effects=True, vmem_limit_bytes=56 * 1024 * 1024),
    )(pattern, density)


def solution(mesh):
    placed = P("row", "col")
    return jax.shard_map(local, mesh=mesh, in_specs=(placed, placed), out_specs=placed, check_vma=False)
```

time: 115 us -> 114 us (level)
  no operation moved by 1% of the time
where the time goes in v3:
time: 114 us
  Pallas kernels  112 us (98%)
  local copies, waits for them, and re-layouts  1.67 us (1%)
    pallas_call x1, Pallas kernels, local(): pl.pallas_call(kernel, out_shape=jax.ShapeDtypeStruct(density.shape, f32)...  112 us

profile of v3, /device:TPU:1, one launch (start us, length us, event | category | flops | bytes accessed | tf_op | source)
XLA Modules:
  0.0 113.7 jit_solution(2810195824876219290)
XLA Ops:
  0.0 112.0 %shard_map.28 = f32[256,256]{1,0:T(8,128)} custom-call(s32[2,2]{1,0:T(2,128)} %pattern_in.1, f32[256,256]{1,0:T(8,128)} %density.1), custom_call_target="tpu_custom_call" | custom-call | tf_op jit(solution)/shard_map/pallas_call | solution.py:345
  112.0 1.7 %copy.4 = f32[256,256]{1,0:T(8,128)} copy(f32[256,256]{1,0:T(8,128)} %shard_map.28) | data formatting | bytes 524288

commit v4 on v3

--- a/solution.py
+++ b/solution.py
@@ -17,10 +17,11 @@
 
 GROUPS = {}
 BEGIN_ROWS = [(0, 2), (1, 2)]
+Z_STEPS = [(1, -1), (1, -1)]
 BEGIN_COLS = (1, -1)
 BEGIN = [(plan, sign) for plan in (0, 1) for sign in (1, -1)]
 
-ROWS64, HOP, SMALL, DOT, DOT_TILE = 1.31, 2.1, 0.03, 0.15, 0.12
+ROWS64, HOP, SMALL, DOT, DOT_TILE = 1.45, 2.2, 0.03, 0.15, 0.12
 NEAR_FIRST = [
     [(0, 0), (1, 0), (-1, 0), (0, 1), (0, -1)],
     [(2, 0), (0, 2), (1, 1), (1, -1), (-1, 1), (-1, -1)],
@@ -74,7 +75,7 @@
     def own_col(s, ts):
         pushes = []
         for t in ts:
-            pushes += [(("z", sign), COL_SIZE, ("col", s, t, sign, "h")) for sign in (1, -1)]
+            pushes += [(("z", step), COL_SIZE, ("col", s, t, step, "h")) for step in Z_STEPS[s]]
         return pushes + [(("core", 0), 0.15, ("col", s, t, 0, "s")) for t in ts]
 
     def overlap(one, other):
@@ -108,10 +109,14 @@
                 pushes = []
                 if dz:
                     sign = 1 if dz > 0 else -1
-                    if abs(dz) < 3:
+                    reach = max(Z_STEPS[s])
+                    last = ("col", s, t, 4, "q0" if sign == 1 else "q1")
+                    if dz != 4 and reach == 1:
+                        pushes.append((("z", sign), COL_SIZE, ("col", s, t, dz + sign, "h")) if abs(dz) < 3
+                                      else (("z", sign), COL_SIZE / 2, last))
+                    elif abs(dz) == 2:
                         pushes.append((("z", sign), COL_SIZE, ("col", s, t, dz + sign, "h")))
-                    elif dz != 4:
-                        pushes.append((("z", sign), COL_SIZE / 2, ("col", s, t, 4, "q0" if sign == 1 else "q1")))
+                        pushes.append((("z", 2 * sign), COL_SIZE / 2, last))
                     pushes.append((("core", 0), 0.15, ("col", s, t, dz, "s")))
                     add(("ring", s, t, dz), 0, 0, col_tile(s, t, dz, False), pushes)
                 before = [("ring", s, t, dz)] if dz else [("start",) if p == 0 else ("final", p - 1, t % 2)]
@@ -180,10 +185,10 @@
         now += cost
         order.append(name)
         times[name] = now
-        for where, amount, piece in pushes:
-            rate = 1.0 if where[0] == "core" else ROWS64
-            free[where] = max(free.get(where, 0.0), now) + amount * rate
-            done(piece, free[where] + HOP)
+        for (axis, steps), amount, piece in pushes:
+            way = axis, steps > 0
+            free[way] = max(free.get(way, 0.0), now) + amount * max(1, abs(steps)) * ROWS64
+            done(piece, free[way] + HOP)
         done(name, now)
     return order, times
 
@@ -226,7 +231,8 @@
     for copy in fetch:
         copy.start()
 
-    peers = [device(dx=1), device(dx=-1), device(dy=1), device(dy=-1), device(dz=1), device(dz=-1), sibling]
+    peers = [device(dx=1), device(dx=-1), device(dy=1), device(dy=-1), sibling]
+    peers += [device(dz=step) for step in (1, -1)]
     barrier = pltpu.get_barrier_semaphore()
     for peer in peers:
         pl.semaphore_signal(barrier, inc=1, device_id=peer, device_id_type=MESH)
@@ -299,19 +305,23 @@
             _, p, o = name[:3]
             low, count, lane, lanes = STREAMS[p + 1][o]
             here, wide = pl.ds(low, count), pl.ds(lane, lanes)
-            term = None
-            for key in GROUPS[name[1:]]:
-                k = k_col(*key) if isinstance(key[1], bool) else k_row(*key)
+            places = [k_col(*key) if isinstance(key[1], bool) else k_row(*key) for key in GROUPS[name[1:]]]
+            if (p, o) not in begun:
+                begun.add((p, o))
+                acc[p, here, wide] = jnp.zeros((count, lanes), f32)
+
+            def one_tile(n, carry):
+                k = places[0]
+                for other in range(1, len(places)):
+                    k = jnp.where(n == other, places[other], k)
                 high_a, low_a = split(rows[p, k, here, :])
                 high_b, low_b = col_hi[p // 2, k, :, wide], col_lo[p // 2, k, :, wide]
-                for one, other in ((high_a, high_b), (high_a, low_b), (low_a, high_b)):
-                    dot = jnp.dot(one, other, preferred_element_type=f32)
-                    term = dot if term is None else term + dot
-            if (p, o) in begun:
-                acc[p, here, wide] += term
-            else:
-                begun.add((p, o))
-                acc[p, here, wide] = term
+                left = jnp.concatenate([high_a, low_a, high_a], axis=1)
+                right = jnp.concatenate([high_b, high_b, low_b], axis=0)
+                acc[p, here, wide] += jnp.dot(left, right, preferred_element_type=f32)
+                return carry
+
+            lax.fori_loop(0, len(places), one_tile, 0)
         elif kind == "final":
             _, p, o = name
             low, count, lane, lanes = STREAMS[p + 1][o]

time: 114 us -> 119 us (1.044)
  Pallas kernels: 112 us -> 118 us
    pallas_call x1, Pallas kernels: 112 us -> 118 us  [local(): pl.pallas_call(kernel, out_shape=jax.ShapeDtypeStruct(density.shape, f32)...]
where the time goes in v4:
time: 119 us
  Pallas kernels  118 us (99%)
  local copies, waits for them, and re-layouts  1.67 us (1%)
    pallas_call x1, Pallas kernels, local(): pl.pallas_call(kernel, out_shape=jax.ShapeDtypeStruct(density.shape, f32)...  118 us

profile of v4, /device:TPU:1, one launch (start us, length us, event | category | flops | bytes accessed | tf_op | source)
XLA Modules:
  0.0 119.3 jit_solution(4747218523696686192)
XLA Ops:
  0.0 117.6 %shard_map.28 = f32[256,256]{1,0:T(8,128)} custom-call(s32[2,2]{1,0:T(2,128)} %pattern_in.1, f32[256,256]{1,0:T(8,128)} %density.1), custom_call_target="tpu_custom_call" | custom-call | tf_op jit(solution)/shard_map/pallas_call | solution.py:355
  117.6 1.7 %copy.4 = f32[256,256]{1,0:T(8,128)} copy(f32[256,256]{1,0:T(8,128)} %shard_map.28) | data formatting | bytes 524288

commit v5 on v4

--- a/solution.py
+++ b/solution.py
@@ -305,23 +305,18 @@
             _, p, o = name[:3]
             low, count, lane, lanes = STREAMS[p + 1][o]
             here, wide = pl.ds(low, count), pl.ds(lane, lanes)
-            places = [k_col(*key) if isinstance(key[1], bool) else k_row(*key) for key in GROUPS[name[1:]]]
-            if (p, o) not in begun:
+            keys = GROUPS[name[1:]]
+            places = [k_col(*key) if isinstance(key[1], bool) else k_row(*key) for key in keys]
+            high_a, low_a = split(jnp.concatenate([rows[p, k, here, :] for k in places], axis=1))
+            high_b = jnp.concatenate([col_hi[p // 2, k, :, wide] for k in places], axis=0)
+            low_b = jnp.concatenate([col_lo[p // 2, k, :, wide] for k in places], axis=0)
+            both = jnp.dot(jnp.concatenate([high_a, low_a], axis=0), high_b, preferred_element_type=f32)
+            term = both[:count] + both[count:] + jnp.dot(high_a, low_b, preferred_element_type=f32)
+            if (p, o) in begun:
+                acc[p, here, wide] += term
+            else:
                 begun.add((p, o))
-                acc[p, here, wide] = jnp.zeros((count, lanes), f32)
-
-            def one_tile(n, carry):
-                k = places[0]
-                for other in range(1, len(places)):
-                    k = jnp.where(n == other, places[other], k)
-                high_a, low_a = split(rows[p, k, here, :])
-                high_b, low_b = col_hi[p // 2, k, :, wide], col_lo[p // 2, k, :, wide]
-                left = jnp.concatenate([high_a, low_a, high_a], axis=1)
-                right = jnp.concatenate([high_b, high_b, low_b], axis=0)
-                acc[p, here, wide] += jnp.dot(left, right, preferred_element_type=f32)
-                return carry
-
-            lax.fori_loop(0, len(places), one_tile, 0)
+                acc[p, here, wide] = term
         elif kind == "final":
             _, p, o = name
             low, count, lane, lanes = STREAMS[p + 1][o]

time: 119 us -> 114 us (0.958)
  Pallas kernels: 118 us -> 112 us
    pallas_call x1, Pallas kernels: 118 us -> 112 us  [local(): pl.pallas_call(kernel, out_shape=jax.ShapeDtypeStruct(density.shape, f32)...]
where the time goes in v5:
time: 114 us
  Pallas kernels  112 us (98%)
  local copies, waits for them, and re-layouts  1.67 us (1%)
    pallas_call x1, Pallas kernels, local(): pl.pallas_call(kernel, out_shape=jax.ShapeDtypeStruct(density.shape, f32)...  112 us

profile of v5, /device:TPU:1, one launch (start us, length us, event | category | flops | bytes accessed | tf_op | source)
XLA Modules:
  0.0 113.8 jit_solution(1382564844264285258)
XLA Ops:
  0.0 112.2 %shard_map.28 = f32[256,256]{1,0:T(8,128)} custom-call(s32[2,2]{1,0:T(2,128)} %pattern_in.1, f32[256,256]{1,0:T(8,128)} %density.1), custom_call_target="tpu_custom_call" | custom-call | tf_op jit(solution)/shard_map/pallas_call | solution.py:350
  112.2 1.7 %copy.4 = f32[256,256]{1,0:T(8,128)} copy(f32[256,256]{1,0:T(8,128)} %shard_map.28) | data formatting | bytes 524288

commit v6 on v5

--- a/solution.py
+++ b/solution.py
@@ -16,12 +16,12 @@
 RING = (0, 1, -1, 2, -2, 3, -3, 4)
 
 GROUPS = {}
-BEGIN_ROWS = [(0, 2), (1, 2)]
-Z_STEPS = [(1, -1), (1, -1)]
-BEGIN_COLS = (1, -1)
-BEGIN = [(plan, sign) for plan in (0, 1) for sign in (1, -1)]
-
-ROWS64, HOP, SMALL, DOT, DOT_TILE = 1.45, 2.2, 0.03, 0.15, 0.12
+BEGIN_ROWS = [(0, "g1"), (1, "g1")]
+COL_SIZE = 1.0
+BEGIN_COLS = ()
+BEGIN = [(0, "g1"), (1, "g1")]
+
+ROWS64, HOP, SMALL, DOT, DOT_TILE = 1.5, 1.8, 0.03, 0.15, 0.12
 NEAR_FIRST = [
     [(0, 0), (1, 0), (-1, 0), (0, 1), (0, -1)],
     [(2, 0), (0, 2), (1, 1), (1, -1), (-1, 1), (-1, -1)],
@@ -35,15 +35,30 @@
 SQUARE = [(0, 128, 0, 128), (0, 128, 128, 128), (128, 128, 0, 256)]
 STREAMS = [HALVES, SQUARE, HALVES, SQUARE, HALVES]
 COLUMNS = [(0, 128, 0, 128), (128, 128, 0, 128), (0, 128, 128, 128), (128, 128, 128, 128)]
-COL_SIZE = 1.0
-
-
-def far_sign(h, plan, a=0):
-    return 1 if (h + plan + (0, 1, 2, 1)[a]) % 2 == 0 else -1
+SLOTS = (0, 1, -1, 2)
+SETS = [((0, 1), (1, 2), (3, 1)), ((0, 1), (1, 3))]
+SET_CHOICE = [[0, 0], [0, 0, 0], [0, 0], [0, 0, 0]]
+FAR = [(0, 1, 0), (0, 1)]
+
+
+def sets_of(p, h):
+    return SETS[SET_CHOICE[p][h]]
+
+
+def far_sign(p, h, plan, group=None):
+    turn = 0 if group is None else FAR[SET_CHOICE[p][h]][group]
+    return 1 if (h + plan + turn) % 2 == 0 else -1
+
+
+def group_of(p, h, a):
+    slot = SLOTS.index(a)
+    return next(n for n, (first, count) in enumerate(sets_of(p, h)) if first <= slot < first + count)
 
 
 def row_tile(p, h, plan, a, b):
-    return [] if (a, b) == (0, 0) else [("row", p, h, plan, a, b, "h")]
+    if (a, b) == (0, 0):
+        return []
+    return [("row", p, h, plan, a if b == 0 else "g%d" % group_of(p, h, a), b)]
 
 
 def col_tile(s, t, dz, other):
@@ -68,14 +83,14 @@
         for axis in (0, 1):
             for plan in (0, 1):
                 for sign in (1, -1):
-                    a, b = (sign, 0) if axis == 0 else (0, sign)
-                    pushes.append((link(plan, axis, sign), row_size(p, h), ("row", p, h, plan, a, b, "h")))
+                    a, b = (sign, 0) if axis == 0 else ("g0", sign)
+                    pushes.append((link(plan, axis, sign), row_size(p, h), ("row", p, h, plan, a, b)))
         return pushes
 
     def own_col(s, ts):
         pushes = []
         for t in ts:
-            pushes += [(("z", step), COL_SIZE, ("col", s, t, step, "h")) for step in Z_STEPS[s]]
+            pushes += [(("z", step), COL_SIZE, ("col", s, t, step, "h")) for step in (1, -1)]
         return pushes + [(("core", 0), 0.15, ("col", s, t, 0, "s")) for t in ts]
 
     def overlap(one, other):
@@ -93,30 +108,27 @@
             size = row_size(p, h)
             for plan in (0, 1):
                 for sign in (1, -1):
-                    for a in (0, 1, -1, 2):
-                        if sign == far_sign(h, plan, a):
-                            add(("pass", p, h, plan, a, sign), 0, 0, row_tile(p, h, plan, a, sign),
-                                [(link(plan, 1, sign), size, ("row", p, h, plan, a, 2, "h"))])
                     pushes = []
-                    if sign == far_sign(h, plan):
-                        pushes = [(link(plan, 0, sign), size, ("row", p, h, plan, 2, 0, "h"))]
-                    pushes += [(link(plan, 1, turn), size, ("row", p, h, plan, sign, turn, "h")) for turn in (1, -1)]
-                    add(("turn", p, h, plan, sign), 0, 0, row_tile(p, h, plan, sign, 0), pushes)
-                pushes = [(link(plan, 1, turn), size, ("row", p, h, plan, 2, turn, "h")) for turn in (1, -1)]
-                add(("turn", p, h, plan, 2), 0, 0, row_tile(p, h, plan, 2, 0), pushes)
+                    if sign == far_sign(p, h, plan):
+                        pushes = [(link(plan, 0, sign), size, ("row", p, h, plan, 2, 0))]
+                        add(("turn", p, h, plan, sign), 0, 0, row_tile(p, h, plan, sign, 0), pushes)
+                for g, (first, count) in enumerate(sets_of(p, h)):
+                    if g:
+                        needs = [piece for a in SLOTS[first:first + count] for piece in row_tile(p, h, plan, a, 0)]
+                        add(("turn", p, h, plan, "g%d" % g), 0, 0, needs, [
+                            (link(plan, 1, turn), size * count, ("row", p, h, plan, "g%d" % g, turn)) for turn in (1, -1)])
+                    sign = far_sign(p, h, plan, g)
+                    add(("pass", p, h, plan, "g%d" % g), 0, 0, [("row", p, h, plan, "g%d" % g, sign)],
+                        [(link(plan, 1, sign), size * count, ("row", p, h, plan, "g%d" % g, 2))])
         if p % 2 == 0:
             for t, dz in ((t, dz) for dz in RING for t in range(4)):
                 pushes = []
                 if dz:
                     sign = 1 if dz > 0 else -1
-                    reach = max(Z_STEPS[s])
-                    last = ("col", s, t, 4, "q0" if sign == 1 else "q1")
-                    if dz != 4 and reach == 1:
-                        pushes.append((("z", sign), COL_SIZE, ("col", s, t, dz + sign, "h")) if abs(dz) < 3
-                                      else (("z", sign), COL_SIZE / 2, last))
-                    elif abs(dz) == 2:
+                    if abs(dz) < 3:
                         pushes.append((("z", sign), COL_SIZE, ("col", s, t, dz + sign, "h")))
-                        pushes.append((("z", 2 * sign), COL_SIZE / 2, last))
+                    elif dz != 4:
+                        pushes.append((("z", sign), COL_SIZE / 2, ("col", s, t, 4, "q0" if sign == 1 else "q1")))
                     pushes.append((("core", 0), 0.15, ("col", s, t, dz, "s")))
                     add(("ring", s, t, dz), 0, 0, col_tile(s, t, dz, False), pushes)
                 before = [("ring", s, t, dz)] if dz else [("start",) if p == 0 else ("final", p - 1, t % 2)]
@@ -205,7 +217,7 @@
     return high, (value - high.astype(f32)).astype(bf16)
 
 
-def kernel(pattern_in, density, out, rows, cols, col_hi, col_lo, acc, pattern,
+def kernel(pattern_in, density, out, wide_rows, half_rows, cols, col_hi, col_lo, acc, pattern,
            row_send, row_recv, col_send, col_recv, local_sem):
     size = density.shape[0]
     r, c = lax.axis_index("row"), lax.axis_index("col")
@@ -223,10 +235,19 @@
     def k_col(dz, other):
         return ((z - dz + NZ) % NZ) * 2 + (1 - core if other else core)
 
+    def stream_of(p, h):
+        before = [h_ for p_ in range(4) for h_, other in enumerate(STREAMS[p_])
+                  if (p_, h_) < (p, h) and other[3] == STREAMS[p][h][3]]
+        return (wide_rows if STREAMS[p][h][3] == size else half_rows).at[len(before)]
+
+    step_rows = HALVES[0][1] // 2
     fetch = [
-        pltpu.make_async_copy(density, rows.at[0, c], local_sem.at[0]),
-        pltpu.make_async_copy(density, cols.at[0, r], local_sem.at[1]),
-        pltpu.make_async_copy(pattern_in, pattern, local_sem.at[2]),
+        pltpu.make_async_copy(density.at[pl.ds((2 * h + plan) * step_rows, step_rows)], stream_of(0, h).at[plan, 0, 0],
+                              local_sem.at[2 * h + plan])
+        for h in (0, 1) for plan in (0, 1)]
+    fetch += [
+        pltpu.make_async_copy(density, cols.at[0, r], local_sem.at[4]),
+        pltpu.make_async_copy(pattern_in, pattern, local_sem.at[5]),
     ]
     for copy in fetch:
         copy.start()
@@ -246,44 +267,51 @@
         parts = [value[:, n:n + BLOCK] * mask[low // BLOCK][(lane + n) // BLOCK] for n in range(0, value.shape[1], BLOCK)]
         return jnp.concatenate(parts, axis=1)
 
-    def copy_of(piece):
-        if piece[0] == "row":
-            _, p, h, plan, a, b, _ = piece
-            low, count, lane, lanes = STREAMS[p][h]
-            here = pl.ds(low + plan * (count // 2), count // 2), pl.ds(lane, lanes)
-            return rows, p, here, row_send.at[p], row_recv.at[ROW[piece]], (a, b) if plan == 0 else (b, a)
+    def slot_of(distance):
+        return distance + distance // 2 - 2 * (distance // 3)
+
+    def gathered(p, low, dx, dy):
+        parts = []
+        for h, stream in enumerate(STREAMS[p]):
+            if stream[0] == low:
+                ref = stream_of(p, h)
+                parts.append(jnp.concatenate([ref[0, slot_of(dy), slot_of(dx)], ref[1, slot_of(dx), slot_of(dy)]], axis=0))
+        return parts[0] if len(parts) == 1 else jnp.concatenate(parts, axis=1)
+
+    def remote(src, dst, send, recv, target):
+        return pltpu.make_async_remote_copy(
+            src_ref=src, dst_ref=dst, send_sem=send, recv_sem=recv, device_id=target, device_id_type=MESH)
+
+    def row_copy(piece, where):
+        _, p, h, plan, a, b = piece
+        ref = stream_of(p, h).at[plan]
+        moved = a if b == 0 else b
+        held = SLOTS.index(0 if abs(moved) == 1 else where[1]) if where else SLOTS.index(moved)
+        if b == 0:
+            src, dst = ref.at[0, held], ref.at[0, SLOTS.index(a)]
+        else:
+            first, count = sets_of(p, h)[int(a[1])]
+            src, dst = ref.at[held, pl.ds(first, count)], ref.at[SLOTS.index(b), pl.ds(first, count)]
+        target = device(**{"d" + where[0]: where[1]}) if where else sibling
+        return remote(src, dst, row_send.at[p], row_recv.at[ROW[piece]], target)
+
+    def col_copy(piece, where):
         _, s, t, dz, part = piece
         low, count, lane, lanes = COLUMNS[t]
         if part in ("q0", "q1"):
             count //= 2
             low += count if part == "q1" else 0
-        here = pl.ds(low, count), pl.ds(lane, lanes)
-        return cols, s, here, col_send.at[s], col_recv.at[COL[piece]], dz
-
-    def push(where, piece):
-        buffer, index, here, send, recv, offset = copy_of(piece)
-        axis, sign = where
-        if piece[0] == "row":
-            dx, dy = offset
-            held = k_row(dx - sign, dy) if axis == "x" else k_row(dx, dy - sign)
+        if not where:
+            held, target = k_col(dz, part == "s"), sibling
+        elif where[0] == "core":
+            held, target = k_col(dz, False), sibling
         else:
-            held = k_col(offset if axis == "core" else offset - sign, False)
-        target = sibling if axis == "core" else device(**{"d" + axis: sign})
-        part = buffer.at[index, held, *here]
-        pltpu.make_async_remote_copy(
-            src_ref=part, dst_ref=part, send_sem=send, recv_sem=recv,
-            device_id=target, device_id_type=MESH).start()
-
-    def wait(piece):
-        buffer, index, here, send, recv, offset = copy_of(piece)
-        if piece[0] == "row":
-            held = k_row(*offset)
-        else:
-            held = k_col(offset, piece[-1] == "s")
-        part = buffer.at[index, held, *here]
-        pltpu.make_async_remote_copy(
-            src_ref=part, dst_ref=part, send_sem=send, recv_sem=recv,
-            device_id=sibling, device_id_type=MESH).wait_recv()
+            held, target = k_col(dz - where[1], False), device(dz=where[1])
+        ref = cols.at[s, held, pl.ds(low, count), pl.ds(lane, lanes)]
+        return remote(ref, ref, col_send.at[s], col_recv.at[COL[piece]], target)
+
+    def copy_of(piece, where=None):
+        return (row_copy if piece[0] == "row" else col_copy)(piece, where)
 
     waited, begun = set(), set()
 
@@ -292,7 +320,7 @@
         for need in needs:
             if need[0] in ("row", "col") and need not in waited:
                 waited.add(need)
-                wait(need)
+                copy_of(need).wait_recv()
         kind = name[0]
         if kind == "split":
             _, s, t, dz, other = name
@@ -306,8 +334,13 @@
             low, count, lane, lanes = STREAMS[p + 1][o]
             here, wide = pl.ds(low, count), pl.ds(lane, lanes)
             keys = GROUPS[name[1:]]
-            places = [k_col(*key) if isinstance(key[1], bool) else k_row(*key) for key in keys]
-            high_a, low_a = split(jnp.concatenate([rows[p, k, here, :] for k in places], axis=1))
+            if isinstance(keys[0][1], bool):
+                places = [k_col(*key) for key in keys]
+                steps = [((x - k % NX + NX) % NX, (y - k // NX + NY) % NY) for k in places]
+            else:
+                places = [k_row(*key) for key in keys]
+                steps = [(dx % NX, dy % NY) for dx, dy in keys]
+            high_a, low_a = split(jnp.concatenate([gathered(p, low, *step) for step in steps], axis=1))
             high_b = jnp.concatenate([col_hi[p // 2, k, :, wide] for k in places], axis=0)
             low_b = jnp.concatenate([col_lo[p // 2, k, :, wide] for k in places], axis=0)
             both = jnp.dot(jnp.concatenate([high_a, low_a], axis=0), high_b, preferred_element_type=f32)
@@ -323,25 +356,28 @@
             here, wide = pl.ds(low, count), pl.ds(lane, lanes)
             value = masked(acc[p, here, wide], low, lane)
             if p % 2:
-                value = 3.0 * rows[p, c, here, wide] - 2.0 * value
+                value = 3.0 * gathered(p, low, 0, 0) - 2.0 * value
             if p == 2 * STEPS - 1:
                 out[here, wide] = value
             else:
-                rows[p + 1, c, here, wide] = value
+                ref = stream_of(p + 1, o)
+                ref[0, 0, 0] = value[:count // 2]
+                ref[1, 0, 0] = value[count // 2:]
                 if p % 2:
                     cols[p // 2 + 1, r, here, wide] = value
         for where, _, piece in pushes:
-            push(where, piece)
+            copy_of(piece, where).start()
 
     for name in ORDER:
         run(name)
 
+    def sent(ref, sem):
+        pltpu.make_async_copy(ref, ref, sem).wait()
+
     for p in range(2 * STEPS):
-        whole = rows.at[p, pl.ds(0, 15)]
-        pltpu.make_async_copy(whole, whole, row_send.at[p]).wait()
+        sent(cols.at[0, pl.ds(0, 15)], row_send.at[p])
     for s in range(STEPS):
-        whole = cols.at[s, pl.ds(0, 15)]
-        pltpu.make_async_copy(whole, whole, col_send.at[s]).wait()
+        sent(cols.at[s, pl.ds(0, 15)], col_send.at[s])
 
 
 def local(density, pattern):
@@ -353,7 +389,8 @@
         in_specs=[pl.BlockSpec(memory_space=pltpu.HBM), pl.BlockSpec(memory_space=pltpu.HBM)],
         out_specs=pl.BlockSpec(memory_space=pltpu.VMEM),
         scratch_shapes=[
-            pltpu.VMEM((2 * STEPS, tiles, size, size), f32),
+            pltpu.VMEM((3 * STEPS, 2, NY, NX, size // 4, size), f32),
+            pltpu.VMEM((2 * STEPS, 2, NY, NX, size // 4, size // 2), f32),
             pltpu.VMEM((STEPS, tiles, size, size), f32),
             pltpu.VMEM((STEPS, tiles, size, size), bf16),
             pltpu.VMEM((STEPS, tiles, size, size), bf16),
@@ -363,7 +400,7 @@
             pltpu.SemaphoreType.DMA((len(ROW),)),
             pltpu.SemaphoreType.DMA((STEPS,)),
             pltpu.SemaphoreType.DMA((len(COL),)),
-            pltpu.SemaphoreType.DMA((3,)),
+            pltpu.SemaphoreType.DMA((6,)),
         ],
         compiler_params=pltpu.CompilerParams(
             collective_id=0, has_side_effects=True, vmem_limit_bytes=56 * 1024 * 1024),

time: 114 us -> 113 us (level)
  no operation moved by 1% of the time
where the time goes in v6:
time: 113 us
  Pallas kernels  111 us (98%)
  local copies, waits for them, and re-layouts  1.67 us (1%)
    pallas_call x1, Pallas kernels, local(): pl.pallas_call(kernel, out_shape=jax.ShapeDtypeStruct(density.shape, f32)...  111 us

profile of v6, /device:TPU:1, one launch (start us, length us, event | category | flops | bytes accessed | tf_op | source)
XLA Modules:
  0.0 112.8 jit_solution(7564844554325231968)
XLA Ops:
  0.0 111.1 %shard_map.28 = f32[256,256]{1,0:T(8,128)} custom-call(s32[2,2]{1,0:T(2,128)} %pattern_in.1, f32[256,256]{1,0:T(8,128)} %density.1), custom_call_target="tpu_custom_call" | custom-call | tf_op jit(solution)/shard_map/pallas_call | solution.py:386
  111.1 1.7 %copy.4 = f32[256,256]{1,0:T(8,128)} copy(f32[256,256]{1,0:T(8,128)} %shard_map.28) | data formatting | bytes 524288

commit v7 on v6

--- a/solution.py
+++ b/solution.py
@@ -21,7 +21,7 @@
 BEGIN_COLS = ()
 BEGIN = [(0, "g1"), (1, "g1")]
 
-ROWS64, HOP, SMALL, DOT, DOT_TILE = 1.5, 1.8, 0.03, 0.15, 0.12
+ROWS64, HOP, SMALL, DOT, DOT_TILE = 1.6, 1.7, 0.015, 0.08, 0.06
 NEAR_FIRST = [
     [(0, 0), (1, 0), (-1, 0), (0, 1), (0, -1)],
     [(2, 0), (0, 2), (1, 1), (1, -1), (-1, 1), (-1, -1)],
@@ -41,6 +41,16 @@
 FAR = [(0, 1, 0), (0, 1)]
 
 
+PAIRED = 2 * STEPS - 1
+CHUNKS = 2
+COLUMN_PARTS = [(0, 2), (1, 3)]
+PAIR_GROUPS = [[(0, 0), (0, 1), (0, -1), (1, 0)], [(0, 2), (1, 1), (1, -1)], [(1, 2)]]
+PAIR_OFFSETS = [key for group in PAIR_GROUPS for key in group]
+MOVE_AFTER = [(0, "g2"), (1, "g2")]
+OWN_AFTER = []
+WAITED = ("row", "col", "pair", "part")
+
+
 def sets_of(p, h):
     return SETS[SET_CHOICE[p][h]]
 
@@ -59,6 +69,13 @@
     if (a, b) == (0, 0):
         return []
     return [("row", p, h, plan, a if b == 0 else "g%d" % group_of(p, h, a), b)]
+
+
+def pair_tile(h, plan, dx, dy):
+    if (dx, dy) == (0, 0):
+        return []
+    name = "near" if plan == 0 and dx == 1 and abs(dy) == 1 else dy
+    return [("pair", h, plan, dx, name)]
 
 
 def col_tile(s, t, dz, other):
@@ -80,6 +97,12 @@
 
     def own_row(p, h):
         pushes = []
+        if p == PAIRED:
+            size = row_size(p, h)
+            pushes = [(("pair", 1), size, ("pair", h, 1, 1, 0))]
+            pushes += [(("y", sign), size, ("pair", h, 0, 0, sign)) for sign in (1, -1)]
+            pushes += [(("pair", 1), size, ("pair", h, 0, 1, 0))]
+            return pushes + [(("y", sign), size, ("pair", h, 1, 0, sign)) for sign in (1, -1)]
         for axis in (0, 1):
             for plan in (0, 1):
                 for sign in (1, -1):
@@ -106,7 +129,7 @@
         s = p // 2
         for h, stream in enumerate(STREAMS[p]):
             size = row_size(p, h)
-            for plan in (0, 1):
+            for plan in (0, 1) if p != PAIRED else ():
                 for sign in (1, -1):
                     pushes = []
                     if sign == far_sign(p, h, plan):
@@ -120,6 +143,37 @@
                     sign = far_sign(p, h, plan, g)
                     add(("pass", p, h, plan, "g%d" % g), 0, 0, [("row", p, h, plan, "g%d" % g, sign)],
                         [(link(plan, 1, sign), size * count, ("row", p, h, plan, "g%d" % g, 2))])
+            if p == PAIRED:
+                turn = far_sign(p, h, 0)
+                add(("pass", p, h, 0, 0), 0, 0, pair_tile(h, 0, 0, turn), [(("y", turn), size, ("pair", h, 0, 0, 2))])
+                add(("turn", p, h, 0, "g1"), 0, 0, pair_tile(h, 0, 0, 1) + pair_tile(h, 0, 0, -1),
+                    [(("pair", 1), 2 * size, ("pair", h, 0, 1, "near"))])
+                add(("turn", p, h, 0, "g2"), 0, 0, pair_tile(h, 0, 0, 2), [(("pair", 1), size, ("pair", h, 0, 1, 2))])
+                add(("turn", p, h, 1, "g1"), 0, 0, pair_tile(h, 1, 1, 0),
+                    [(("y", sign), size, ("pair", h, 1, 1, sign)) for sign in (1, -1)])
+                for dx in (0, 1):
+                    turn = far_sign(p, h, 1) * (1 - 2 * dx)
+                    add(("pass", p, h, 1, dx), 0, 0, pair_tile(h, 1, dx, turn), [(("y", turn), size, ("pair", h, 1, dx, 2))])
+        if p == PAIRED - 1:
+            for e in range(CHUNKS):
+                size = 4.0 / CHUNKS
+                begun = ("final", p - 1, e)
+                add(("move", e), 1.5, SMALL, [begun] + [("turn", p, 1, *key) for key in MOVE_AFTER],
+                    [(("mate", 1), size / 2, ("moved", e))])
+                add(("own", e), 0, SMALL, [begun, ("moved", e)] + [("ring", s, t, dz) for t, dz in OWN_AFTER], [
+                    (("z", 1), size, ("e", e, 0)), (("z", -1), size, ("e", e, 1)), (("core", 0), 0.15 * size, ("shared", e, 3))])
+                near = [("ring", s, t, dz) for t in COLUMN_PARTS[e] for dz in (3, -3, 4)]
+                add(("lend", e), 1.5, SMALL, near, [(("mate", 1), size / (n - 1), ("lent", e, n)) for n in (2, 3)])
+                for n in range(4):
+                    came = ("e" if n < 2 else "lent", e, n)
+                    if n < 2:
+                        pushes = [(("z", 1 - 2 * n), size / 2, ("e2", e, n)), (("core", 0), 0.15 * size, ("shared", e, n))]
+                    else:
+                        pushes = [(("core", 0), 0.15 * size, ("shared", e, n))] if n == 2 else []
+                    add(("slot", e, n), 0, SMALL, [came], pushes)
+                    after = [("slot", e, n)] + ([("own", e)] if n == 3 else [])
+                    add(("esplit", e, n, False), 2, 2 * SMALL, after)
+                    add(("esplit", e, n, True), 2, 2 * SMALL, [("shared", e, n)] + after)
         if p % 2 == 0:
             for t, dz in ((t, dz) for dz in RING for t in range(4)):
                 pushes = []
@@ -137,15 +191,19 @@
         for o, target in enumerate(STREAMS[p + 1]):
             rows_used = [h for h, stream in enumerate(STREAMS[p]) if overlap(stream, (target[0], target[1], 0, 256))]
             cols_used = [t for t, col in enumerate(COLUMNS) if overlap(col, (0, 256, target[2], target[3]))]
-            pieces = {key: [piece for h in rows_used
-                            for piece in row_tile(p, h, 0, *key) + row_tile(p, h, 1, *key[::-1])] for key in OFFSETS}
+            if p == PAIRED:
+                pieces = {key: [piece for h in rows_used for plan in (0, 1) for piece in pair_tile(h, plan, *key)]
+                          for key in PAIR_OFFSETS}
+            else:
+                pieces = {key: [piece for h in rows_used
+                                for piece in row_tile(p, h, 0, *key) + row_tile(p, h, 1, *key[::-1])] for key in OFFSETS}
             starts = [("start",) if p == 0 else ("final", p - 1, h) for h in rows_used]
             if p % 2 == 0 and target[0] == 0:
                 need = [piece for key in OFFSETS for piece in pieces[key]] + starts
                 groups = [[(dz, other) for dz in group for other in (False, True)] for group in COL_GROUPS]
                 needs = [need + [("split", s, t, *key) for t in cols_used for key in group] for group in groups]
             else:
-                groups = NEAR_FIRST
+                groups = PAIR_GROUPS if p == PAIRED else NEAR_FIRST
                 need = [("split", s, t, dz, other) for t in cols_used for dz in RING for other in (False, True)]
                 needs = [[piece for key in group for piece in pieces[key]] + starts + (need if p % 2 == 0 else [])
                          for group in groups]
@@ -157,6 +215,12 @@
             if p < 2 * STEPS - 1:
                 pushes = own_row(p + 1, o) + (own_col(s + 1, (o, 2 + o)) if p % 2 else [])
             macs = [("mac", p, o, n) for n in range(len(groups))]
+            if p == PAIRED:
+                extra = [("esplit", e, n, other) for e in range(CHUNKS) for n in range(4) for other in (False, True)]
+                for n, group in enumerate(groups):
+                    jobs[("macx", p, o, n)] = (3.5 + p, DOT + DOT_TILE * len(group), needs[n] + extra, [])
+                add(("give", o), 1, SMALL, [("macx", p, o, n) for n in range(len(groups))], [(("mate", 1), 2.0, ("part", o))])
+                macs.append(("part", o))
             if p % 2 == 0 and o == 2:
                 add(("final", p, o), 1, 2 * SMALL, macs)
                 add(("begin", p, o), 1, 0, [("final", p, o)] + [("turn", p + 1, 1, *key) for key in BEGIN], pushes)
@@ -198,9 +262,9 @@
         order.append(name)
         times[name] = now
         for (axis, steps), amount, piece in pushes:
-            way = axis, steps > 0
+            way = {"pair": ("x", True), "mate": ("x", False)}.get(axis, (axis, steps > 0))
             free[way] = max(free.get(way, 0.0), now) + amount * max(1, abs(steps)) * ROWS64
-            done(piece, free[way] + HOP)
+            done(piece, free[way] + HOP * (3.5 if piece[0] == "e" else 1))
         done(name, now)
     return order, times
 
@@ -209,6 +273,7 @@
 ORDER, TIMES = make_order(JOBS)
 PIECES = [piece for name in JOBS for _, _, piece in JOBS[name][3]]
 ROW = {name: n for n, name in enumerate(piece for piece in PIECES if piece[0] == "row")}
+PAIR = {name: n for n, name in enumerate(piece for piece in PIECES if piece[0] == "pair")}
 COL = {name: n for n, name in enumerate(piece for piece in PIECES if piece[0] == "col")}
 
 
@@ -217,8 +282,9 @@
     return high, (value - high.astype(f32)).astype(bf16)
 
 
-def kernel(pattern_in, density, out, wide_rows, half_rows, cols, col_hi, col_lo, acc, pattern,
-           row_send, row_recv, col_send, col_recv, local_sem):
+def kernel(pattern_in, density, out, wide_rows, half_rows, cols, col_hi, col_lo, acc, extra, extra_hi, extra_lo,
+           partial, landed, pattern, row_send, row_recv, pair_recv, col_send, col_recv, part_send, part_recv, move_send, move_recv,
+           ring_send, ring_recv, lend_send, lend_recv, share_send, share_recv, local_sem):
     size = density.shape[0]
     r, c = lax.axis_index("row"), lax.axis_index("col")
     z, core = r // 2, r % 2
@@ -276,6 +342,14 @@
             if stream[0] == low:
                 ref = stream_of(p, h)
                 parts.append(jnp.concatenate([ref[0, slot_of(dy), slot_of(dx)], ref[1, slot_of(dx), slot_of(dy)]], axis=0))
+        return parts[0] if len(parts) == 1 else jnp.concatenate(parts, axis=1)
+
+    def gathered_pair(low, dx, dy):
+        parts = []
+        for h, stream in enumerate(STREAMS[PAIRED]):
+            if stream[0] == low:
+                ref = stream_of(PAIRED, h)
+                parts.append(jnp.concatenate([ref[plan, dx, slot_of(dy)] for plan in (0, 1)], axis=0))
         return parts[0] if len(parts) == 1 else jnp.concatenate(parts, axis=1)
 
     def remote(src, dst, send, recv, target):
@@ -310,15 +384,67 @@
         ref = cols.at[s, held, pl.ds(low, count), pl.ds(lane, lanes)]
         return remote(ref, ref, col_send.at[s], col_recv.at[COL[piece]], target)
 
+    inward = 1 - 2 * (x % 2)
+    mate = device(dx=-inward)
+    odd = (z + x // 2) % 2
+    count_e = size // CHUNKS
+
+    def k_pair(dx, dy):
+        return ((y - dy + NY) % NY) * NX + (x + inward if dx else x)
+
+    def pair_copy(piece, where):
+        _, h, plan, dx, dy = piece
+        ref = stream_of(PAIRED, h).at[plan]
+        if dy == "near":
+            src, dst = ref.at[0, pl.ds(1, 2)], ref.at[1, pl.ds(1, 2)]
+        elif where and where[0] == "pair":
+            src, dst = ref.at[0, SLOTS.index(dy)], ref.at[1, SLOTS.index(dy)]
+        else:
+            held = 0 if abs(dy) < 2 else where[1] if where else 2
+            src, dst = ref.at[dx, SLOTS.index(held)], ref.at[dx, SLOTS.index(dy)]
+        target = sibling
+        if where:
+            target = device(dx=inward) if where[0] == "pair" else device(dy=where[1])
+        return remote(src, dst, row_send.at[PAIRED], pair_recv.at[PAIR[piece]], target)
+
+    def part_copy(piece, where):
+        here = pl.ds(piece[1] * (size // 2), size // 2)
+        return remote(partial.at[here], landed.at[here], part_send.at[0], part_recv.at[piece[1]], mate)
+
+    def slot_rows(n):
+        offset = (odd - 2, 2 - odd, 4 + odd, 3 * odd)[n]
+        return ((z + offset + NZ) % NZ) // 2
+
+    def extra_part(e, n, other):
+        index = slot_rows(n) * 2 + (1 - core if other else core)
+        return extra.at[index, pl.ds(e * count_e, count_e)]
+
+    def ring_copy(e, n, ref):
+        return remote(ref, ref, ring_send.at[0], ring_recv.at[e * 2 + n], device(dz=1 - 2 * n))
+
+    def share_copy(e, n, other=False):
+        ref = extra_part(e, n, other)
+        return remote(ref, ref, share_send.at[0], share_recv.at[e * 4 + n], sibling)
+
+    def move_copy(e):
+        here = pl.ds(e * count_e, count_e)
+        return remote(cols.at[1, r, here], extra.at[(z // 2) * 2 + core, here], move_send.at[0], move_recv.at[e], mate)
+
+    def lend_copy(e, n):
+        z_from = (z + (5 - odd if n == 2 else 3)) % NZ
+        here = pl.ds(e * count_e, count_e)
+        return remote(cols.at[1, z_from * 2 + core, here], extra.at[(z_from // 2) * 2 + core, here], lend_send.at[0],
+                      lend_recv.at[e * 2 + n - 2], mate)
+
     def copy_of(piece, where=None):
-        return (row_copy if piece[0] == "row" else col_copy)(piece, where)
+        return {"row": row_copy, "col": col_copy, "pair": pair_copy, "part": part_copy}[piece[0]](piece, where)
 
     waited, begun = set(), set()
 
     def run(name):
         _, _, needs, pushes = JOBS[name]
         for need in needs:
-            if need[0] in ("row", "col") and need not in waited:
+            if need[0] in WAITED and need not in waited:
                 waited.add(need)
                 copy_of(need).wait_recv()
         kind = name[0]
@@ -329,32 +455,90 @@
             high, low = split(cols[s, k, *here])
             col_hi[s, k, *here] = high
             col_lo[s, k, *here] = low
-        elif kind == "mac":
+        elif kind == "move":
+            @pl.when(odd == 1)
+            def _():
+                move_copy(name[1]).start()
+        elif kind == "own":
+            e = name[1]
+
+            @pl.when(odd == 0)
+            def _():
+                move_copy(e).wait_recv()
+                ring_copy(e, 0, extra_part(e, 3, False)).start()
+                ring_copy(e, 1, extra_part(e, 3, False)).start()
+                share_copy(e, 3).start()
+        elif kind == "slot":
+            _, e, n = name
+            if n < 2:
+                ring_copy(e, n, extra_part(e, n, False)).wait_recv()
+
+                @pl.when(odd == 1)
+                def _():
+                    ring_copy(e, n, extra_part(e, n, False)).start()
+
+                share_copy(e, n).start()
+            elif n == 2:
+                lend_copy(e, 2).wait_recv()
+                share_copy(e, 2).start()
+            else:
+                @pl.when(odd == 1)
+                def _():
+                    lend_copy(e, 3).wait_recv()
+                    share_copy(e, 3).start()
+        elif kind == "lend":
+            lend_copy(name[1], 2).start()
+
+            @pl.when(odd == 0)
+            def _():
+                lend_copy(name[1], 3).start()
+        elif kind == "esplit":
+            _, e, n, other = name
+            if other:
+                share_copy(e, n, True).wait_recv()
+            here = pl.ds(e * count_e, count_e)
+            index = slot_rows(n) * 2 + (1 - core if other else core)
+            high, low = split(extra[index, here, :])
+            extra_hi[index, here, :] = high
+            extra_lo[index, here, :] = low
+        elif kind in ("mac", "macx"):
             _, p, o = name[:3]
             low, count, lane, lanes = STREAMS[p + 1][o]
             here, wide = pl.ds(low, count), pl.ds(lane, lanes)
-            keys = GROUPS[name[1:]]
-            if isinstance(keys[0][1], bool):
+            keys = GROUPS[p, o, name[3]]
+            if p == PAIRED:
+                places = [k_pair(*key) for key in keys]
+                tiles = [gathered_pair(low, dx, dy % NY) for dx, dy in keys]
+            elif isinstance(keys[0][1], bool):
                 places = [k_col(*key) for key in keys]
-                steps = [((x - k % NX + NX) % NX, (y - k // NX + NY) % NY) for k in places]
+                tiles = [gathered(p, low, (x - k % NX + NX) % NX, (y - k // NX + NY) % NY) for k in places]
             else:
                 places = [k_row(*key) for key in keys]
-                steps = [(dx % NX, dy % NY) for dx, dy in keys]
-            high_a, low_a = split(jnp.concatenate([gathered(p, low, *step) for step in steps], axis=1))
-            high_b = jnp.concatenate([col_hi[p // 2, k, :, wide] for k in places], axis=0)
-            low_b = jnp.concatenate([col_lo[p // 2, k, :, wide] for k in places], axis=0)
+                tiles = [gathered(p, low, dx % NX, dy % NY) for dx, dy in keys]
+            high_a, low_a = split(jnp.concatenate(tiles, axis=1))
+            if kind == "mac":
+                high_b = jnp.concatenate([col_hi[p // 2, k, :, wide] for k in places], axis=0)
+                low_b = jnp.concatenate([col_lo[p // 2, k, :, wide] for k in places], axis=0)
+            else:
+                places = [(k // NX) * 2 + k % 2 for k in places]
+                high_b = jnp.concatenate([extra_hi[k] for k in places], axis=0)
+                low_b = jnp.concatenate([extra_lo[k] for k in places], axis=0)
             both = jnp.dot(jnp.concatenate([high_a, low_a], axis=0), high_b, preferred_element_type=f32)
             term = both[:count] + both[count:] + jnp.dot(high_a, low_b, preferred_element_type=f32)
-            if (p, o) in begun:
-                acc[p, here, wide] += term
-            else:
-                begun.add((p, o))
-                acc[p, here, wide] = term
+            total, at = (acc, (p, here, wide)) if kind == "mac" else (partial, (here, wide))
+            if (kind, p, o) in begun:
+                total[at] += term
+            else:
+                begun.add((kind, p, o))
+                total[at] = term
         elif kind == "final":
             _, p, o = name
             low, count, lane, lanes = STREAMS[p + 1][o]
             here, wide = pl.ds(low, count), pl.ds(lane, lanes)
-            value = masked(acc[p, here, wide], low, lane)
+            value = acc[p, here, wide]
+            if p == PAIRED:
+                value += landed[here, wide]
+            value = masked(value, low, lane)
             if p % 2:
                 value = 3.0 * gathered(p, low, 0, 0) - 2.0 * value
             if p == 2 * STEPS - 1:
@@ -366,7 +550,8 @@
                 if p % 2:
                     cols[p // 2 + 1, r, here, wide] = value
         for where, _, piece in pushes:
-            copy_of(piece, where).start()
+            if piece[0] in WAITED:
+                copy_of(piece, where).start()
 
     for name in ORDER:
         run(name)
@@ -375,14 +560,27 @@
         pltpu.make_async_copy(ref, ref, sem).wait()
 
     for p in range(2 * STEPS):
-        sent(cols.at[0, pl.ds(0, 15)], row_send.at[p])
+        sent(cols.at[0, pl.ds(0, 7 if p == PAIRED else 15)], row_send.at[p])
     for s in range(STEPS):
         sent(cols.at[s, pl.ds(0, 15)], col_send.at[s])
+    sent(partial, part_send.at[0])
+    sent(extra.at[pl.ds(0, 4)], share_send.at[0])
+    sent(extra.at[pl.ds(0, 2)], ring_send.at[0])
+
+    @pl.when(odd == 0)
+    def _():
+        sent(extra.at[pl.ds(0, 2)], lend_send.at[0])
+
+    @pl.when(odd == 1)
+    def _():
+        sent(extra.at[0], lend_send.at[0])
+        sent(extra.at[0], move_send.at[0])
 
 
 def local(density, pattern):
     size = density.shape[0]
     tiles = NX * NY
+    dma = pltpu.SemaphoreType.DMA
     return pl.pallas_call(
         kernel,
         out_shape=jax.ShapeDtypeStruct(density.shape, f32),
@@ -395,12 +593,20 @@
             pltpu.VMEM((STEPS, tiles, size, size), bf16),
             pltpu.VMEM((STEPS, tiles, size, size), bf16),
             pltpu.VMEM((2 * STEPS, size, size), f32),
+            pltpu.VMEM((tiles // 2, size, size), f32),
+            pltpu.VMEM((tiles // 2, size, size), bf16),
+            pltpu.VMEM((tiles // 2, size, size), bf16),
+            pltpu.VMEM((size, size), f32),
+            pltpu.VMEM((size, size), f32),
             pltpu.SMEM(pattern.shape, jnp.int32),
-            pltpu.SemaphoreType.DMA((2 * STEPS,)),
-            pltpu.SemaphoreType.DMA((len(ROW),)),
-            pltpu.SemaphoreType.DMA((STEPS,)),
-            pltpu.SemaphoreType.DMA((len(COL),)),
-            pltpu.SemaphoreType.DMA((6,)),
+            dma((2 * STEPS,)), dma((len(ROW),)), dma((len(PAIR),)),
+            dma((STEPS,)), dma((len(COL),)),
+            dma((1,)), dma((2,)),
+            dma((1,)), dma((CHUNKS,)),
+            dma((1,)), dma((CHUNKS * 2,)),
+            dma((1,)), dma((CHUNKS * 2,)),
+            dma((1,)), dma((CHUNKS * 4,)),
+            dma((6,)),
         ],
         compiler_params=pltpu.CompilerParams(
             collective_id=0, has_side_effects=True, vmem_limit_bytes=56 * 1024 * 1024),

time: 113 us -> 120 us (1.062)
  Pallas kernels: 111 us -> 118 us
    pallas_call x1, Pallas kernels: 111 us -> 118 us  [local(): pl.pallas_call(kernel, out_shape=jax.ShapeDtypeStruct(density.shape, f32)...]
where the time goes in v7:
time: 120 us
  Pallas kernels  118 us (98%)
  local copies, waits for them, and re-layouts  1.67 us (1%)
    pallas_call x1, Pallas kernels, local(): pl.pallas_call(kernel, out_shape=jax.ShapeDtypeStruct(density.shape, f32)...  118 us

profile of v7, /device:TPU:1, one launch (start us, length us, event | category | flops | bytes accessed | tf_op | source)
XLA Modules:
  0.0 120.0 jit_solution(4632434572908985540)
XLA Ops:
  0.0 118.4 %shard_map.28 = f32[256,256]{1,0:T(8,128)} custom-call(s32[2,2]{1,0:T(2,128)} %pattern_in.1, f32[256,256]{1,0:T(8,128)} %density.1), custom_call_target="tpu_custom_call" | custom-call | tf_op jit(solution)/shard_map/pallas_call | solution.py:584
  118.4 1.7 %copy.4 = f32[256,256]{1,0:T(8,128)} copy(f32[256,256]{1,0:T(8,128)} %shard_map.28) | data formatting | bytes 524288

commit v8 on v6

--- a/solution.py
+++ b/solution.py
@@ -16,12 +16,12 @@
 RING = (0, 1, -1, 2, -2, 3, -3, 4)
 
 GROUPS = {}
-BEGIN_ROWS = [(0, "g1"), (1, "g1")]
+BEGIN_ROWS = ["g2"]
 COL_SIZE = 1.0
-BEGIN_COLS = ()
-BEGIN = [(0, "g1"), (1, "g1")]
-
-ROWS64, HOP, SMALL, DOT, DOT_TILE = 1.5, 1.8, 0.03, 0.15, 0.12
+BEGIN_COLS = (1, -1)
+BEGIN = ["g1"]
+
+ROWS64, HOP, SMALL, DOT, DOT_TILE = 1.45, 2.0, 0.03, 0.1, 0.1
 NEAR_FIRST = [
     [(0, 0), (1, 0), (-1, 0), (0, 1), (0, -1)],
     [(2, 0), (0, 2), (1, 1), (1, -1), (-1, 1), (-1, -1)],
@@ -35,6 +35,7 @@
 SQUARE = [(0, 128, 0, 128), (0, 128, 128, 128), (128, 128, 0, 256)]
 STREAMS = [HALVES, SQUARE, HALVES, SQUARE, HALVES]
 COLUMNS = [(0, 128, 0, 128), (128, 128, 0, 128), (0, 128, 128, 128), (128, 128, 128, 128)]
+AXES = {(axis, sign): (("first", "second")[axis], sign) for axis in (0, 1) for sign in (1, -1)}
 SLOTS = (0, 1, -1, 2)
 SETS = [((0, 1), (1, 2), (3, 1)), ((0, 1), (1, 3))]
 SET_CHOICE = [[0, 0], [0, 0, 0], [0, 0], [0, 0, 0]]
@@ -45,9 +46,9 @@
     return SETS[SET_CHOICE[p][h]]
 
 
-def far_sign(p, h, plan, group=None):
+def far_sign(p, h, group=None):
     turn = 0 if group is None else FAR[SET_CHOICE[p][h]][group]
-    return 1 if (h + plan + turn) % 2 == 0 else -1
+    return 1 if (h + turn) % 2 == 0 else -1
 
 
 def group_of(p, h, a):
@@ -55,10 +56,10 @@
     return next(n for n, (first, count) in enumerate(sets_of(p, h)) if first <= slot < first + count)
 
 
-def row_tile(p, h, plan, a, b):
+def row_tile(p, h, a, b):
     if (a, b) == (0, 0):
         return []
-    return [("row", p, h, plan, a if b == 0 else "g%d" % group_of(p, h, a), b)]
+    return [("row", p, h, a if b == 0 else "g%d" % group_of(p, h, a), b)]
 
 
 def col_tile(s, t, dz, other):
@@ -72,19 +73,15 @@
 def make_jobs():
     jobs = {}
 
-    def link(plan, axis, sign):
-        return ("x" if (axis == 0) == (plan == 0) else "y", sign)
-
     def row_size(p, h):
         return STREAMS[p][h][1] * STREAMS[p][h][3] / (128 * 256)
 
     def own_row(p, h):
         pushes = []
         for axis in (0, 1):
-            for plan in (0, 1):
-                for sign in (1, -1):
-                    a, b = (sign, 0) if axis == 0 else ("g0", sign)
-                    pushes.append((link(plan, axis, sign), row_size(p, h), ("row", p, h, plan, a, b)))
+            for sign in (1, -1):
+                a, b = (sign, 0) if axis == 0 else ("g0", sign)
+                pushes.append((AXES[axis, sign], row_size(p, h), ("row", p, h, a, b)))
         return pushes
 
     def own_col(s, ts):
@@ -100,26 +97,22 @@
         jobs[name] = (priority, cost + SMALL * (len(pushes) + len(needs)), needs, list(pushes))
 
     add(("start",), 0, SMALL, [], own_row(0, 0) + own_col(0, (0, 1)))
-    add(("begin", 0, 1), 0, 0, [("turn", 0, 0, *key) for key in BEGIN_ROWS], own_row(0, 1))
+    add(("begin", 0, 1), 0, 0, [("turn", 0, 0, key) for key in BEGIN_ROWS], own_row(0, 1))
     add(("begin_col",), 0, 0, [("ring", 0, t, dz) for t in (0, 1) for dz in BEGIN_COLS], own_col(0, (2, 3)))
     for p in range(2 * STEPS):
         s = p // 2
         for h, stream in enumerate(STREAMS[p]):
             size = row_size(p, h)
-            for plan in (0, 1):
-                for sign in (1, -1):
-                    pushes = []
-                    if sign == far_sign(p, h, plan):
-                        pushes = [(link(plan, 0, sign), size, ("row", p, h, plan, 2, 0))]
-                        add(("turn", p, h, plan, sign), 0, 0, row_tile(p, h, plan, sign, 0), pushes)
-                for g, (first, count) in enumerate(sets_of(p, h)):
-                    if g:
-                        needs = [piece for a in SLOTS[first:first + count] for piece in row_tile(p, h, plan, a, 0)]
-                        add(("turn", p, h, plan, "g%d" % g), 0, 0, needs, [
-                            (link(plan, 1, turn), size * count, ("row", p, h, plan, "g%d" % g, turn)) for turn in (1, -1)])
-                    sign = far_sign(p, h, plan, g)
-                    add(("pass", p, h, plan, "g%d" % g), 0, 0, [("row", p, h, plan, "g%d" % g, sign)],
-                        [(link(plan, 1, sign), size * count, ("row", p, h, plan, "g%d" % g, 2))])
+            sign = far_sign(p, h)
+            add(("turn", p, h, "far"), 0, 0, row_tile(p, h, sign, 0), [(AXES[0, sign], size, ("row", p, h, 2, 0))])
+            for g, (first, count) in enumerate(sets_of(p, h)):
+                if g:
+                    needs = [piece for a in SLOTS[first:first + count] for piece in row_tile(p, h, a, 0)]
+                    add(("turn", p, h, "g%d" % g), 0, 0, needs, [
+                        (AXES[1, turn], size * count, ("row", p, h, "g%d" % g, turn)) for turn in (1, -1)])
+                sign = far_sign(p, h, g)
+                add(("pass", p, h, "g%d" % g), 0, 0, [("row", p, h, "g%d" % g, sign)],
+                    [(AXES[1, sign], size * count, ("row", p, h, "g%d" % g, 2))])
         if p % 2 == 0:
             for t, dz in ((t, dz) for dz in RING for t in range(4)):
                 pushes = []
@@ -137,8 +130,7 @@
         for o, target in enumerate(STREAMS[p + 1]):
             rows_used = [h for h, stream in enumerate(STREAMS[p]) if overlap(stream, (target[0], target[1], 0, 256))]
             cols_used = [t for t, col in enumerate(COLUMNS) if overlap(col, (0, 256, target[2], target[3]))]
-            pieces = {key: [piece for h in rows_used
-                            for piece in row_tile(p, h, 0, *key) + row_tile(p, h, 1, *key[::-1])] for key in OFFSETS}
+            pieces = {key: [piece for h in rows_used for piece in row_tile(p, h, *key)] for key in OFFSETS}
             starts = [("start",) if p == 0 else ("final", p - 1, h) for h in rows_used]
             if p % 2 == 0 and target[0] == 0:
                 need = [piece for key in OFFSETS for piece in pieces[key]] + starts
@@ -159,7 +151,7 @@
             macs = [("mac", p, o, n) for n in range(len(groups))]
             if p % 2 == 0 and o == 2:
                 add(("final", p, o), 1, 2 * SMALL, macs)
-                add(("begin", p, o), 1, 0, [("final", p, o)] + [("turn", p + 1, 1, *key) for key in BEGIN], pushes)
+                add(("begin", p, o), 1, 0, [("final", p, o)] + [("turn", p + 1, 1, key) for key in BEGIN], pushes)
             else:
                 add(("final", p, o), 1, 2 * SMALL, macs, pushes)
     return jobs
@@ -198,7 +190,7 @@
         order.append(name)
         times[name] = now
         for (axis, steps), amount, piece in pushes:
-            way = axis, steps > 0
+            way = "z" if axis == "z" else "core" if axis == "core" else "xy", steps > 0
             free[way] = max(free.get(way, 0.0), now) + amount * max(1, abs(steps)) * ROWS64
             done(piece, free[way] + HOP)
         done(name, now)
@@ -229,7 +221,11 @@
 
     sibling = (z * 2 + 1 - core, c)
 
-    def k_row(dx, dy):
+    def turned(a, b):
+        return a * (1 - core) + b * core, b * (1 - core) + a * core
+
+    def k_row(a, b):
+        dx, dy = turned(a, b)
         return ((y - dy + NY) % NY) * NX + (x - dx + NX) % NX
 
     def k_col(dz, other):
@@ -240,14 +236,10 @@
                   if (p_, h_) < (p, h) and other[3] == STREAMS[p][h][3]]
         return (wide_rows if STREAMS[p][h][3] == size else half_rows).at[len(before)]
 
-    step_rows = HALVES[0][1] // 2
-    fetch = [
-        pltpu.make_async_copy(density.at[pl.ds((2 * h + plan) * step_rows, step_rows)], stream_of(0, h).at[plan, 0, 0],
-                              local_sem.at[2 * h + plan])
-        for h in (0, 1) for plan in (0, 1)]
+    fetch = [pltpu.make_async_copy(density.at[pl.ds(*HALVES[h][:2])], stream_of(0, h).at[0, 0], local_sem.at[h]) for h in (0, 1)]
     fetch += [
-        pltpu.make_async_copy(density, cols.at[0, r], local_sem.at[4]),
-        pltpu.make_async_copy(pattern_in, pattern, local_sem.at[5]),
+        pltpu.make_async_copy(density, cols.at[0, r], local_sem.at[2]),
+        pltpu.make_async_copy(pattern_in, pattern, local_sem.at[3]),
     ]
     for copy in fetch:
         copy.start()
@@ -270,12 +262,11 @@
     def slot_of(distance):
         return distance + distance // 2 - 2 * (distance // 3)
 
-    def gathered(p, low, dx, dy):
+    def gathered(p, low, a, b):
         parts = []
         for h, stream in enumerate(STREAMS[p]):
             if stream[0] == low:
-                ref = stream_of(p, h)
-                parts.append(jnp.concatenate([ref[0, slot_of(dy), slot_of(dx)], ref[1, slot_of(dx), slot_of(dy)]], axis=0))
+                parts.append(stream_of(p, h)[slot_of(b), slot_of(a)])
         return parts[0] if len(parts) == 1 else jnp.concatenate(parts, axis=1)
 
     def remote(src, dst, send, recv, target):
@@ -283,8 +274,8 @@
             src_ref=src, dst_ref=dst, send_sem=send, recv_sem=recv, device_id=target, device_id_type=MESH)
 
     def row_copy(piece, where):
-        _, p, h, plan, a, b = piece
-        ref = stream_of(p, h).at[plan]
+        _, p, h, a, b = piece
+        ref = stream_of(p, h)
         moved = a if b == 0 else b
         held = SLOTS.index(0 if abs(moved) == 1 else where[1]) if where else SLOTS.index(moved)
         if b == 0:
@@ -292,7 +283,10 @@
         else:
             first, count = sets_of(p, h)[int(a[1])]
             src, dst = ref.at[held, pl.ds(first, count)], ref.at[SLOTS.index(b), pl.ds(first, count)]
-        target = device(**{"d" + where[0]: where[1]}) if where else sibling
+        target = sibling
+        if where:
+            dx, dy = turned(where[1], 0) if where[0] == "first" else turned(0, where[1])
+            target = device(dx=dx, dy=dy)
         return remote(src, dst, row_send.at[p], row_recv.at[ROW[piece]], target)
 
     def col_copy(piece, where):
@@ -336,10 +330,10 @@
             keys = GROUPS[name[1:]]
             if isinstance(keys[0][1], bool):
                 places = [k_col(*key) for key in keys]
-                steps = [((x - k % NX + NX) % NX, (y - k // NX + NY) % NY) for k in places]
+                steps = [turned((x - k % NX + NX) % NX, (y - k // NX + NY) % NY) for k in places]
             else:
                 places = [k_row(*key) for key in keys]
-                steps = [(dx % NX, dy % NY) for dx, dy in keys]
+                steps = [(a % NX, b % NY) for a, b in keys]
             high_a, low_a = split(jnp.concatenate([gathered(p, low, *step) for step in steps], axis=1))
             high_b = jnp.concatenate([col_hi[p // 2, k, :, wide] for k in places], axis=0)
             low_b = jnp.concatenate([col_lo[p // 2, k, :, wide] for k in places], axis=0)
@@ -361,8 +355,7 @@
                 out[here, wide] = value
             else:
                 ref = stream_of(p + 1, o)
-                ref[0, 0, 0] = value[:count // 2]
-                ref[1, 0, 0] = value[count // 2:]
+                ref[0, 0] = value
                 if p % 2:
                     cols[p // 2 + 1, r, here, wide] = value
         for where, _, piece in pushes:
@@ -389,8 +382,8 @@
         in_specs=[pl.BlockSpec(memory_space=pltpu.HBM), pl.BlockSpec(memory_space=pltpu.HBM)],
         out_specs=pl.BlockSpec(memory_space=pltpu.VMEM),
         scratch_shapes=[
-            pltpu.VMEM((3 * STEPS, 2, NY, NX, size // 4, size), f32),
-            pltpu.VMEM((2 * STEPS, 2, NY, NX, size // 4, size // 2), f32),
+            pltpu.VMEM((3 * STEPS, NY, NX, size // 2, size), f32),
+            pltpu.VMEM((2 * STEPS, NY, NX, size // 2, size // 2), f32),
             pltpu.VMEM((STEPS, tiles, size, size), f32),
             pltpu.VMEM((STEPS, tiles, size, size), bf16),
             pltpu.VMEM((STEPS, tiles, size, size), bf16),
@@ -400,7 +393,7 @@
             pltpu.SemaphoreType.DMA((len(ROW),)),
             pltpu.SemaphoreType.DMA((STEPS,)),
             pltpu.SemaphoreType.DMA((len(COL),)),
-            pltpu.SemaphoreType.DMA((6,)),
+            pltpu.SemaphoreType.DMA((4,)),
         ],
         compiler_params=pltpu.CompilerParams(
             collective_id=0, has_side_effects=True, vmem_limit_bytes=56 * 1024 * 1024),

time: 113 us -> 117 us (1.035)
  Pallas kernels: 111 us -> 114 us
    pallas_call x1, Pallas kernels: 111 us -> 114 us  [local(): pl.pallas_call(kernel, out_shape=jax.ShapeDtypeStruct(density.shape, f32)...]
where the time goes in v8:
time: 117 us; the launch traced here: 116 us
  Pallas kernels  114 us (97%)
  local copies, waits for them, and re-layouts  1.67 us (1%)
    pallas_call x1, Pallas kernels, local(): pl.pallas_call(kernel, out_shape=jax.ShapeDtypeStruct(density.shape, f32)...  114 us

profile of v8, /device:TPU:1, one launch (start us, length us, event | category | flops | bytes accessed | tf_op | source)
XLA Modules:
  0.0 115.8 jit_solution(13442259136689705946)
XLA Ops:
  0.0 114.1 %shard_map.28 = f32[256,256]{1,0:T(8,128)} custom-call(s32[2,2]{1,0:T(2,128)} %pattern_in.1, f32[256,256]{1,0:T(8,128)} %density.1), custom_call_target="tpu_custom_call" | custom-call | tf_op jit(solution)/shard_map/pallas_call | solution.py:379
  114.1 1.7 %copy.4 = f32[256,256]{1,0:T(8,128)} copy(f32[256,256]{1,0:T(8,128)} %shard_map.28) | data formatting | bytes 524288

commit v9 on v0

v9 whole, which is shorter than its diff:
```python
import heapq

import jax
import jax.numpy as jnp
from jax import lax
from jax.experimental import pallas as pl
from jax.experimental.pallas import tpu as pltpu
from jax.sharding import PartitionSpec as P

BLOCK = 128
STEPS = 2
NX, NY, NZ = 4, 4, 8
MESH = pl.DeviceIdType.MESH
f32, bf16 = jnp.float32, jnp.bfloat16
OFFSETS = [(dx, dy) for dx in (0, 1, -1, 2) for dy in (0, 1, -1, 2)]
RING = (0, 1, -1, 2, -2, 3, -3, 4)
LAST = 2 * STEPS - 1
GROUPS = {}

ROWS64, HOP, SMALL, DOT, DOT_TILE = 1.4, 2.2, 0.03, 0.15, 0.08
ON_CHIP = 0.3
BEGIN_ROWS = ["g1"]
BEGIN = ["g1"]
NEAR_FIRST = [
    [(0, 0), (1, 0), (-1, 0), (0, 1), (0, -1)],
    [(2, 0), (0, 2), (1, 1), (1, -1), (-1, 1), (-1, -1)],
    [(1, 2), (-1, 2), (2, 1), (2, -1)],
    [(2, 2)],
]
COL_GROUPS = [[0, 1, -1], [2, -2], [3, -3], [4]]
SLOTS = (0, 1, -1, 2)
SETS = [(0, 1), (1, 2), (3, 1)]
FAR = (0, 1, 0)


def far_sign(h, plan, group=None):
    turn = 0 if group is None else FAR[group]
    return 1 if (h + plan + turn) % 2 == 0 else -1


def group_of(a):
    slot = SLOTS.index(a)
    return next(n for n, (first, count) in enumerate(SETS) if first <= slot < first + count)


def row_tile(p, h, plan, a, b):
    if (a, b) == (0, 0):
        return []
    return [("row", p, h, plan, a if b == 0 else "g%d" % group_of(a), b)]


def col_tile(s, t, dz, cc):
    if dz == 0:
        return []
    return [("col", s, t, dz, part, cc) for part in (("q0", "q1") if dz == 4 else ("h",))]


def make_jobs():
    jobs = {}

    def link(plan, axis, sign):
        return ("x" if (axis == 0) == (plan == 0) else "y", sign)

    def own_row(p, h, plans=(0, 1)):
        pushes = []
        for axis in (0, 1):
            for plan in plans:
                for sign in (1, -1):
                    a, b = (sign, 0) if axis == 0 else ("g0", sign)
                    pushes.append((link(plan, axis, sign), 1.0, ("row", p, h, plan, a, b)))
        return pushes

    def own_col(s, cc, ts):
        size = 0.5 if s else 1.0
        return [(("z", sign), size, ("col", s, t, sign, "h", cc)) for t in ts for sign in (1, -1)]

    def add(name, priority, cost, needs, pushes=()):
        jobs[name] = (priority, cost + SMALL * (len(pushes) + len(needs)), needs, list(pushes))

    add(("start",), 0, SMALL, [], [(("core", 0), ON_CHIP, ("init", n)) for n in range(4)]
        + own_row(0, 0, (0,)) + own_col(0, None, (0, 1)))
    add(("start_rows",), 0, 0, [("init", 0)], own_row(0, 0, (1,)))
    add(("start_cols",), 0, 0, [("init", 2)], own_col(0, None, (2, 3)))
    add(("begin", 0, 1), 0, 0, [("init", 1)] + [("turn", 0, 0, plan, key) for plan in (0, 1) for key in BEGIN_ROWS], own_row(0, 1))
    for p in range(2 * STEPS):
        s = p // 2
        for h in (0, 1):
            for plan in (0, 1):
                sign = far_sign(h, plan)
                add(("turn", p, h, plan, "far"), 0, 0, row_tile(p, h, plan, sign, 0),
                    [(link(plan, 0, sign), 1.0, ("row", p, h, plan, 2, 0))])
                for g, (first, count) in enumerate(SETS):
                    if g:
                        needs = [piece for a in SLOTS[first:first + count] for piece in row_tile(p, h, plan, a, 0)]
                        add(("turn", p, h, plan, "g%d" % g), 0, 0, needs, [
                            (link(plan, 1, turn), count, ("row", p, h, plan, "g%d" % g, turn)) for turn in (1, -1)])
                    sign = far_sign(h, plan, g)
                    add(("pass", p, h, plan, "g%d" % g), 0, 0, [("row", p, h, plan, "g%d" % g, sign)],
                        [(link(plan, 1, sign), count, ("row", p, h, plan, "g%d" % g, 2))])
        cores = [None] if s == 0 else [0, 1]
        if p % 2 == 0:
            for cc in cores:
                size = 0.5 if s else 1.0
                if s:
                    add(("begin_col", cc), 0, 0, [("final", p - 1, cc)], own_col(s, cc, range(4)))
                for t, dz in ((t, dz) for dz in RING for t in range(4)):
                    pushes = []
                    if dz:
                        sign = 1 if dz > 0 else -1
                        if abs(dz) < 3:
                            pushes.append((("z", sign), size, ("col", s, t, dz + sign, "h", cc)))
                        elif dz != 4:
                            pushes.append((("z", sign), size / 2, ("col", s, t, 4, "q0" if sign == 1 else "q1", cc)))
                        add(("ring", s, t, dz, cc), 0, 0, col_tile(s, t, dz, cc), pushes)
                    first = ("begin_col", cc) if s else ("start",) if t < 2 else ("start_cols",)
                    add(("split", s, t, dz, cc), 2, SMALL, [("ring", s, t, dz, cc)] if dz else [first])
        for o in (0, 1):
            pieces = {key: row_tile(p, o, 0, *key) + row_tile(p, o, 1, *key[::-1]) for key in OFFSETS}
            if p == 0:
                begun = [("start_rows",)] if o == 0 else [("begin", 0, 1)]
            else:
                begun = [("final", p - 1, o)]
            if p % 2 == 0 and o == 0:
                need = [piece for key in OFFSETS for piece in pieces[key]] + begun
                groups = [[(dz, plan == 1) for dz in group for plan in (0, 1)] for group in COL_GROUPS]
                needs = [need + [("split", s, 2 * other + n, dz, cc) for dz, other in group for n in (0, 1) for cc in cores]
                         for group in groups]
            else:
                groups = NEAR_FIRST
                need = [("split", s, t, dz, cc) for t in range(4) for dz in RING for cc in cores] if p % 2 == 0 else []
                needs = [[piece for key in group for piece in pieces[key]] + begun + need for group in groups]
            for n, group in enumerate(groups):
                jobs[("mac", p, o, n)] = (4 + p, DOT + DOT_TILE * len(group), needs[n], [])
                GROUPS[p, o, n] = group
            add(("give", p, o), 1, SMALL, [("mac", p, o, n) for n in range(len(groups))], [(("core", 0), 2 * ON_CHIP, ("given", p, o))])
            extra = [("squared", o)] if p == LAST else []
            add(("final", p, o), 1, 3 * SMALL, [("give", p, o), ("given", p, o)] + extra)
            if p == LAST:
                continue
            if p % 2 == 0 and o:
                gate = [("turn", p + 1, 0, plan, key) for plan in (0, 1) for key in BEGIN]
            else:
                gate = []
            add(("go", p, o), 1, 0, [("final", p, o)] + gate, own_row(p + 1, o))
            if p == LAST - 1:
                add(("square", o), 3, SMALL, [("final", p, o)], [(("core", 0), ON_CHIP, ("squared", o))])
    return jobs


def make_order(jobs):
    ready_at, missing, users = {}, {}, {}
    for name, (_, _, needs, _) in jobs.items():
        missing[name] = len(set(needs))
        ready_at[name] = 0.0
        for need in set(needs):
            users.setdefault(need, []).append(name)
    waiting, ready, free, brought = [], [], {}, set()
    rank = {name: n for n, name in enumerate(jobs)}

    def done(thing, when):
        if thing in brought:
            return
        brought.add(thing)
        for user in users.get(thing, ()):
            missing[user] -= 1
            ready_at[user] = max(ready_at[user], when)
            if missing[user] == 0:
                heapq.heappush(waiting, (ready_at[user], rank[user], user))

    for name in jobs:
        if missing[name] == 0:
            heapq.heappush(waiting, (0.0, rank[name], name))
    now, order, times = 0.0, [], {}
    while waiting or ready:
        if not ready and waiting[0][0] > now:
            now = waiting[0][0]
        while waiting and waiting[0][0] <= now:
            when, number, name = heapq.heappop(waiting)
            heapq.heappush(ready, (jobs[name][0], when, number, name))
        name = heapq.heappop(ready)[-1]
        _, cost, _, pushes = jobs[name]
        now += cost
        order.append(name)
        times[name] = now
        for (axis, steps), amount, piece in pushes:
            way = axis, steps > 0
            free[way] = max(free.get(way, 0.0), now) + amount * ROWS64
            done(piece, free[way] + HOP)
        done(name, now)
    return order, times


JOBS = make_jobs()
ORDER, TIMES = make_order(JOBS)
PIECES = [piece for name in JOBS for _, _, piece in JOBS[name][3]]
ROW = {name: n for n, name in enumerate(piece for piece in PIECES if piece[0] == "row")}
COL = {name: n for n, name in enumerate(dict.fromkeys(piece[:5] for piece in PIECES if piece[0] == "col"))}


def split(value):
    high = value.astype(bf16)
    return high, (value - high.astype(f32)).astype(bf16)


def kernel(pattern_in, density, out, rows, cols, col_hi, col_lo, acc, landed, square, mask, pattern,
           row_send, row_recv, col_send, col_recv, init_send, init_recv, give_send, give_recv, square_send, square_recv, local_sem):
    half = density.shape[0] // 2
    r, c = lax.axis_index("row"), lax.axis_index("col")
    z, core = r // 2, r % 2
    y, x = c // NX, c % NX
    other = 1 - core

    def device(dx=0, dy=0, dz=0):
        return (((z + dz + NZ) % NZ) * 2 + core, ((y + dy + NY) % NY) * NX + (x + dx + NX) % NX)

    sibling = (z * 2 + other, c)

    def remote(src, dst, send, recv, target):
        return pltpu.make_async_remote_copy(
            src_ref=src, dst_ref=dst, send_sem=send, recv_sem=recv, device_id=target, device_id_type=MESH)

    def k_row(dx, dy):
        return ((y - dy + NY) % NY) * NX + (x - dx + NX) % NX

    def k_col(dz, plan):
        return ((z - dz + NZ) % NZ) * 2 + (other if plan else core)

    def place(p, h, plan, b, a):
        return ((p * 2 + h) * 2 + plan) * 16 + b * 4 + a

    lanes = pl.ds(pl.multiple_of(core * half, half), half)
    lanes_other = pl.ds(pl.multiple_of(other * half, half), half)
    mine = pl.ds(pl.multiple_of(core * half, half), half)
    theirs = pl.ds(pl.multiple_of(other * half, half), half)
    fetch = [pltpu.make_async_copy(density.at[pl.ds(h * half, half), lanes], rows.at[place(0, h, 0, 0, 0)], local_sem.at[h])
             for h in (0, 1)]
    fetch += [
        pltpu.make_async_copy(density.at[mine], cols.at[0, r], local_sem.at[2]),
        pltpu.make_async_copy(pattern_in, pattern, local_sem.at[3]),
    ]
    for copy in fetch:
        copy.start()

    peers = [device(dx=1), device(dx=-1), device(dy=1), device(dy=-1), device(dz=1), device(dz=-1), sibling]
    barrier = pltpu.get_barrier_semaphore()
    for peer in peers:
        pl.semaphore_signal(barrier, inc=1, device_id=peer, device_id_type=MESH)
    pl.semaphore_wait(barrier, len(peers))
    for copy in fetch:
        copy.wait()
    for h in (0, 1):
        for g in (0, 1):
            mask[0, h, g] = jnp.full((8, half), pattern[h, g].astype(f32), f32)

    def init_copy(n):
        if n < 2:
            src, dst = density.at[pl.ds(n * half, half), lanes_other], rows.at[place(0, n, 1, 0, 0)]
        elif n == 2:
            src, dst = density.at[theirs], cols.at[0, r]
        else:
            src, dst = mask.at[0], mask.at[1]
        return remote(src, dst, init_send.at[n], init_recv.at[n], sibling)

    def init_wait(n):
        dst = (rows.at[place(0, n, 1, 0, 0)] if n < 2 else cols.at[0, z * 2 + other] if n == 2 else mask.at[1])
        remote(dst, dst, init_send.at[n], init_recv.at[n], sibling).wait_recv()

    def slot_of(distance):
        return distance + distance // 2 - 2 * (distance // 3)

    def gathered(p, h, dx, dy):
        a, b = slot_of(dx), slot_of(dy)
        return jnp.concatenate([rows[place(p, h, 0, b, a)], rows[place(p, h, 1, a, b)]], axis=0)

    def row_copy(piece, where):
        _, p, h, plan, a, b = piece
        moved = a if b == 0 else b
        held = SLOTS.index(0 if abs(moved) == 1 else where[1]) if where else SLOTS.index(moved)
        if b == 0:
            src, dst = rows.at[place(p, h, plan, 0, held)], rows.at[place(p, h, plan, 0, SLOTS.index(a))]
        else:
            first, count = SETS[int(a[1])]
            src = rows.at[pl.ds(place(p, h, plan, held, first), count)]
            dst = rows.at[pl.ds(place(p, h, plan, SLOTS.index(b), first), count)]
        target = device(**{"d" + where[0]: where[1]}) if where else sibling
        return remote(src, dst, row_send.at[p], row_recv.at[ROW[piece]], target)

    def col_copy(piece, where):
        _, s, t, dz, part, _ = piece
        count = half // 2
        low = (t % 2) * count
        if part != "h":
            count //= 2
            low += count if part == "q1" else 0
        held = k_col(dz - where[1] if where else dz, t // 2)
        ref = cols.at[s, held, pl.ds(low, count)]
        return remote(ref, ref, col_send.at[s], col_recv.at[COL[piece[:5]]], device(dz=where[1]) if where else sibling)

    def give_copy(p, o, plan, whole):
        src, dst = acc.at[p, o, plan], landed.at[p, o, 1 - plan]
        if not whole:
            src, dst = src.at[other], dst.at[other]
        return remote(src, dst, give_send.at[p], give_recv.at[(p * 2 + o) * 2 + 1 - plan], sibling)

    def given_wait(p, o, plan, whole):
        dst = landed.at[p, o, plan]
        if not whole:
            dst = dst.at[core]
        remote(dst, dst, give_send.at[p], give_recv.at[(p * 2 + o) * 2 + plan], sibling).wait_recv()

    def square_copy(h):
        return remote(square.at[1, h, 1, h], square.at[1, h, 0, h], square_send.at[0], square_recv.at[h], sibling)

    def summed(p, o, plan, g):
        return (acc[p, o, plan, g] + landed[p, o, plan, g]) * mask[plan, o, g, 0:1, :]

    waited, begun = set(), set()

    def run_job(name):
        kind = name[0]
        needs, pushes = JOBS[name][2:]
        for need in needs:
            if need[0] in ("row", "col") and need not in waited:
                waited.add(need)
                (row_copy if need[0] == "row" else col_copy)(need, None).wait_recv()
            if need[0] == "init" and need not in waited:
                waited.add(need)
                init_wait(need[1])
        if kind == "split":
            _, s, t, dz, _ = name
            k = k_col(dz, t // 2)
            here = pl.ds((t % 2) * (half // 2), half // 2)
            high, low = split(cols[s, k, here, :])
            col_hi[s, k, here, :] = high
            col_lo[s, k, here, :] = low
        elif kind == "mac":
            _, p, o, _ = name
            keys = GROUPS[name[1:]]
            if isinstance(keys[0][1], bool):
                places = [k_col(*key) for key in keys]
                tiles = [gathered(p, o, (x - k % NX + NX) % NX, (y - k // NX + NY) % NY) for k in places]
            else:
                places = [k_row(*key) for key in keys]
                tiles = [gathered(p, o, dx % NX, dy % NY) for dx, dy in keys]
            high_a, low_a = split(jnp.concatenate(tiles, axis=1))
            high_b = jnp.concatenate([col_hi[p // 2, k] for k in places], axis=0)
            low_b = jnp.concatenate([col_lo[p // 2, k] for k in places], axis=0)
            term = (jnp.dot(high_a, high_b, preferred_element_type=f32) + jnp.dot(low_a, high_b, preferred_element_type=f32)
                    + jnp.dot(high_a, low_b, preferred_element_type=f32))
            for plan in (0, 1):
                for g in (0, 1):
                    part = term[plan * half:(plan + 1) * half, g * half:(g + 1) * half]
                    acc[p, o, plan, g] = acc[p, o, plan, g] + part if (p, o) in begun else part
            begun.add((p, o))
        elif kind == "give":
            _, p, o = name
            if p == LAST:
                give_copy(p, o, 1, True).start()
            else:
                @pl.when(core == o)
                def _():
                    for plan in (0, 1):
                        give_copy(p, o, plan, False).start()

                @pl.when(core != o)
                def _():
                    for plan in (0, 1):
                        give_copy(p, o, plan, True).start()
        elif kind == "final":
            _, p, o = name
            s = p // 2
            here = pl.ds(o * half, half)
            if ("mask",) not in waited:
                waited.add(("mask",))
                init_wait(3)
            if p == LAST:
                given_wait(p, o, 0, True)

                @pl.when(core != o)
                def _():
                    remote(square.at[1, o, 0, o], square.at[1, o, 0, o], square_send.at[0], square_recv.at[o], sibling).wait_recv()

                for g in (0, 1):
                    out[here, pl.ds(g * half, half)] = 3.0 * square[s, o, 0, g] - 2.0 * summed(p, o, 0, g)
                return

            def value_of(plan, g):
                value = summed(p, o, plan, g)
                if p % 2:
                    return 3.0 * square[s, o, plan, g] - 2.0 * value
                square[s, o, plan, g] = value
                return value

            @pl.when(core == o)
            def _():
                for plan in (0, 1):
                    given_wait(p, o, plan, True)
                    for g in (0, 1):
                        value = value_of(plan, g)
                        if g == o:
                            rows[place(p + 1, o, plan, 0, 0)] = value
                        if p % 2:
                            cols[s + 1, k_col(0, plan), :, pl.ds(g * half, half)] = value

            @pl.when(core != o)
            def _():
                for plan in (0, 1):
                    given_wait(p, o, plan, False)
                    rows[place(p + 1, o, plan, 0, 0)] = value_of(plan, 1 - o)
        elif kind == "square":
            h = name[1]

            @pl.when(core == h)
            def _():
                square_copy(h).start()
        for where, _, piece in pushes:
            if piece[0] == "row":
                row_copy(piece, where).start()
            elif piece[0] == "col":
                col_copy(piece, where).start()
            elif piece[0] == "init":
                init_copy(piece[1]).start()

    def run(name):
        cc = name[-1] if name[0] in ("ring", "split", "begin_col") else None
        if cc is None:
            run_job(name)
        else:
            @pl.when(core == cc)
            def _():
                run_job(name)

    for name in ORDER:
        run(name)

    def sent(ref, sem):
        pltpu.make_async_copy(ref, ref, sem).wait()

    for n in (0, 1):
        sent(rows.at[0], init_send.at[n])
    sent(cols.at[0, 0], init_send.at[2])
    sent(mask.at[0], init_send.at[3])
    for p in range(2 * STEPS):
        sent(rows.at[pl.ds(0, 60)], row_send.at[p])
        sent(rows.at[pl.ds(0, 4 if p == LAST else 6)], give_send.at[p])
    for s in range(STEPS):
        sent(rows.at[pl.ds(0, 28)], col_send.at[s])
    sent(rows.at[0], square_send.at[0])


def local(density, pattern):
    size = density.shape[0]
    half = size // 2
    tiles = NX * NY
    phases = 2 * STEPS
    dma = pltpu.SemaphoreType.DMA
    return pl.pallas_call(
        kernel,
        out_shape=jax.ShapeDtypeStruct(density.shape, f32),
        in_specs=[pl.BlockSpec(memory_space=pl.ANY), pl.BlockSpec(memory_space=pl.ANY)],
        out_specs=pl.BlockSpec(memory_space=pltpu.VMEM),
        scratch_shapes=[
            pltpu.VMEM((phases * 4 * tiles, half, half), f32),
            pltpu.VMEM((STEPS, tiles, half, size), f32),
            pltpu.VMEM((STEPS, tiles, half, size), bf16),
            pltpu.VMEM((STEPS, tiles, half, size), bf16),
            pltpu.VMEM((phases, 2, 2, 2, half, half), f32),
            pltpu.VMEM((phases, 2, 2, 2, half, half), f32),
            pltpu.VMEM((STEPS, 2, 2, 2, half, half), f32),
            pltpu.VMEM((2, 2, 2, 8, half), f32),
            pltpu.SMEM(pattern.shape, jnp.int32),
            dma((phases,)), dma((len(ROW),)),
            dma((STEPS,)), dma((len(COL),)),
            dma((4,)), dma((4,)),
            dma((phases,)), dma((phases * 4,)),
            dma((1,)), dma((2,)),
            dma((4,)),
        ],
        compiler_params=pltpu.CompilerParams(
            collective_id=0, has_side_effects=True, vmem_limit_bytes=56 * 1024 * 1024),
    )(pattern, density)


def solution(mesh):
    placed = P("row", "col")
    return jax.shard_map(local, mesh=mesh, in_specs=(placed, placed), out_specs=placed, check_vma=False)
```

time: 385 us -> 123 us (0.32)
  waiting for transfers between devices: 339 us -> 0 us
  Pallas kernels: 0 us -> 121 us
  matrix products: 31.1 us -> 0 us
  between operations: 13.5 us -> 0.01 us
    all_gather x6 -> x0, waiting for transfers between devices: 337 us -> none  [the longest x2 128 us: local(): lax.all_gather(current, 'col', axis=1, tiled=True)]
    pallas_call x0 -> x1, Pallas kernels: none -> 121 us  [local(): pl.pallas_call(kernel, out_shape=jax.ShapeDtypeStruct(density.shape, f32)...]
    dot_general x4 -> x0, matrix products: 31.1 us -> none  [accumulate(): jnp.dot(piece, column_block, precision=lax.Precision.HIGHEST, preferred_e...]
  transfers between devices with their start and end apart: 6 -> 0, of which waited for: 6 -> 0; matrix products, arithmetic and copies ran while one was open for 0% -> 0% of each run, Pallas kernels for 0% -> 0%
where the time goes in v9:
time: 123 us
  Pallas kernels  121 us (98%)
  local copies, waits for them, and re-layouts  1.67 us (1%)
    pallas_call x1, Pallas kernels, local(): pl.pallas_call(kernel, out_shape=jax.ShapeDtypeStruct(density.shape, f32)...  121 us

profile of v9, /device:TPU:1, one launch (start us, length us, event | category | flops | bytes accessed | tf_op | source)
XLA Modules:
  0.0 123.1 jit_solution(1421452080018025347)
XLA Ops:
  0.0 121.4 %shard_map.28 = f32[256,256]{1,0:T(8,128)} custom-call(s32[2,2]{1,0:T(2,128)} %pattern_in.1, f32[256,256]{1,0:T(8,128)} %density.1), custom_call_target="tpu_custom_call" | custom-call | tf_op jit(solution)/shard_map/pallas_call | solution.py:457
  121.4 1.7 %copy.4 = f32[256,256]{1,0:T(8,128)} copy(f32[256,256]{1,0:T(8,128)} %shard_map.28) | data formatting | bytes 524288

commit v10 on v6

--- a/solution.py
+++ b/solution.py
@@ -18,10 +18,12 @@
 GROUPS = {}
 BEGIN_ROWS = [(0, "g1"), (1, "g1")]
 COL_SIZE = 1.0
-BEGIN_COLS = ()
+BEGIN_COLS = {}
+LATER_COLS = {}
+DIRECT = set()
 BEGIN = [(0, "g1"), (1, "g1")]
 
-ROWS64, HOP, SMALL, DOT, DOT_TILE = 1.5, 1.8, 0.03, 0.15, 0.12
+ROWS64, HOP, SMALL, DOT, DOT_TILE = 1.4, 2.2, 0.02, 0.1, 0.1
 NEAR_FIRST = [
     [(0, 0), (1, 0), (-1, 0), (0, 1), (0, -1)],
     [(2, 0), (0, 2), (1, 1), (1, -1), (-1, 1), (-1, -1)],
@@ -90,7 +92,7 @@
     def own_col(s, ts):
         pushes = []
         for t in ts:
-            pushes += [(("z", step), COL_SIZE, ("col", s, t, step, "h")) for step in (1, -1)]
+            pushes += [(("z", step), COL_SIZE, ("col", s, t, step, "h")) for step in ((1, -1, 2, -2) if (s, t) in DIRECT else (1, -1))]
         return pushes + [(("core", 0), 0.15, ("col", s, t, 0, "s")) for t in ts]
 
     def overlap(one, other):
@@ -99,9 +101,13 @@
     def add(name, priority, cost, needs, pushes=()):
         jobs[name] = (priority, cost + SMALL * (len(pushes) + len(needs)), needs, list(pushes))
 
-    add(("start",), 0, SMALL, [], own_row(0, 0) + own_col(0, (0, 1)))
+    add(("start",), 0, SMALL, [], own_row(0, 0) + own_col(0, [t for t in range(4) if t not in BEGIN_COLS]))
     add(("begin", 0, 1), 0, 0, [("turn", 0, 0, *key) for key in BEGIN_ROWS], own_row(0, 1))
-    add(("begin_col",), 0, 0, [("ring", 0, t, dz) for t in (0, 1) for dz in BEGIN_COLS], own_col(0, (2, 3)))
+    for t, (behind, dz) in BEGIN_COLS.items():
+        add(("begin_col", t), 0, 0, [("ring", 0, behind, sign * dz) for sign in (1, -1)], own_col(0, (t,)))
+    for t, (behind, dz) in LATER_COLS.items():
+        begun = ("final", 1, COLUMNS[t][0] // 128)
+        add(("later_col", t), 0, 0, [begun] + [("ring", 1, behind, sign * dz) for sign in (1, -1)], own_col(1, (t,)))
     for p in range(2 * STEPS):
         s = p // 2
         for h, stream in enumerate(STREAMS[p]):
@@ -125,7 +131,11 @@
                 pushes = []
                 if dz:
                     sign = 1 if dz > 0 else -1
-                    if abs(dz) < 3:
+                    if (s, t) in DIRECT:
+                        if abs(dz) == 2:
+                            pushes.append((("z", sign), COL_SIZE, ("col", s, t, dz + sign, "h")))
+                            pushes.append((("z", 2 * sign), COL_SIZE / 2, ("col", s, t, 4, "q0" if sign == 1 else "q1")))
+                    elif abs(dz) < 3:
                         pushes.append((("z", sign), COL_SIZE, ("col", s, t, dz + sign, "h")))
                     elif dz != 4:
                         pushes.append((("z", sign), COL_SIZE / 2, ("col", s, t, 4, "q0" if sign == 1 else "q1")))
@@ -155,7 +165,7 @@
                 GROUPS[p, o, n] = group
             pushes = []
             if p < 2 * STEPS - 1:
-                pushes = own_row(p + 1, o) + (own_col(s + 1, (o, 2 + o)) if p % 2 else [])
+                pushes = own_row(p + 1, o) + (own_col(s + 1, [t for t in (o, 2 + o) if t not in LATER_COLS]) if p % 2 else [])
             macs = [("mac", p, o, n) for n in range(len(groups))]
             if p % 2 == 0 and o == 2:
                 add(("final", p, o), 1, 2 * SMALL, macs)
@@ -253,7 +263,7 @@
         copy.start()
 
     peers = [device(dx=1), device(dx=-1), device(dy=1), device(dy=-1), sibling]
-    peers += [device(dz=step) for step in (1, -1)]
+    peers += [device(dz=step) for step in ((1, -1, 2, -2) if DIRECT else (1, -1))]
     barrier = pltpu.get_barrier_semaphore()
     for peer in peers:
         pl.semaphore_signal(barrier, inc=1, device_id=peer, device_id_type=MESH)

time: 113 us -> 113 us (level)
  no operation moved by 1% of the time
where the time goes in v10:
time: 113 us
  Pallas kernels  111 us (98%)
  local copies, waits for them, and re-layouts  1.67 us (1%)
    pallas_call x1, Pallas kernels, local(): pl.pallas_call(kernel, out_shape=jax.ShapeDtypeStruct(density.shape, f32)...  111 us

profile of v10, /device:TPU:1, one launch (start us, length us, event | category | flops | bytes accessed | tf_op | source)
XLA Modules:
  0.0 112.9 jit_solution(9565837839655366529)
XLA Ops:
  0.0 111.3 %shard_map.28 = f32[256,256]{1,0:T(8,128)} custom-call(s32[2,2]{1,0:T(2,128)} %pattern_in.1, f32[256,256]{1,0:T(8,128)} %density.1), custom_call_target="tpu_custom_call" | custom-call | tf_op jit(solution)/shard_map/pallas_call | solution.py:396
  111.3 1.7 %copy.4 = f32[256,256]{1,0:T(8,128)} copy(f32[256,256]{1,0:T(8,128)} %shard_map.28) | data formatting | bytes 524288

commit v11 on v10

--- a/solution.py
+++ b/solution.py
@@ -268,12 +268,12 @@
     for peer in peers:
         pl.semaphore_signal(barrier, inc=1, device_id=peer, device_id_type=MESH)
     pl.semaphore_wait(barrier, len(peers))
-    for copy in fetch:
-        copy.wait()
-
-    mask = [[pattern[a, b].astype(f32) for b in range(2)] for a in range(2)]
+    mask = []
 
     def masked(value, low, lane):
+        if not mask:
+            fetch[-1].wait()
+            mask.extend([pattern[a, b].astype(f32) for b in range(2)] for a in range(2))
         parts = [value[:, n:n + BLOCK] * mask[low // BLOCK][(lane + n) // BLOCK] for n in range(0, value.shape[1], BLOCK)]
         return jnp.concatenate(parts, axis=1)
 
@@ -301,7 +301,10 @@
             src, dst = ref.at[0, held], ref.at[0, SLOTS.index(a)]
         else:
             first, count = sets_of(p, h)[int(a[1])]
-            src, dst = ref.at[held, pl.ds(first, count)], ref.at[SLOTS.index(b), pl.ds(first, count)]
+            here = pl.ds(first, count) if count > 1 else first
+            src, dst = ref.at[held, here], ref.at[SLOTS.index(b), here]
+        if where and p == 0 and held == 0 and (b == 0 or a == "g0"):
+            src = density.at[pl.ds((2 * h + plan) * step_rows, step_rows)]
         target = device(**{"d" + where[0]: where[1]}) if where else sibling
         return remote(src, dst, row_send.at[p], row_recv.at[ROW[piece]], target)
 
@@ -317,7 +320,10 @@
             held, target = k_col(dz, False), sibling
         else:
             held, target = k_col(dz - where[1], False), device(dz=where[1])
-        ref = cols.at[s, held, pl.ds(low, count), pl.ds(lane, lanes)]
+        here = pl.ds(low, count), pl.ds(lane, lanes)
+        ref = cols.at[s, held, *here]
+        if where and s == 0 and dz in ((0,) if where[0] == "core" else (where[1],)):
+            return remote(density.at[*here], ref, col_send.at[s], col_recv.at[COL[piece]], target)
         return remote(ref, ref, col_send.at[s], col_recv.at[COL[piece]], target)
 
     def copy_of(piece, where=None):
@@ -377,6 +383,9 @@
                     cols[p // 2 + 1, r, here, wide] = value
         for where, _, piece in pushes:
             copy_of(piece, where).start()
+        if kind == "start":
+            for copy in fetch[:-1]:
+                copy.wait()
 
     for name in ORDER:
         run(name)
@@ -413,7 +422,7 @@
             pltpu.SemaphoreType.DMA((6,)),
         ],
         compiler_params=pltpu.CompilerParams(
-            collective_id=0, has_side_effects=True, vmem_limit_bytes=56 * 1024 * 1024),
+            collective_id=0, has_side_effects=True, vmem_limit_bytes=53 * 1024 * 1024 + 512 * 1024),
     )(pattern, density)
 
 

time: 113 us -> 112 us (level)
  no operation moved by 1% of the time
where the time goes in v11:
time: 112 us
  Pallas kernels  111 us (99%)
  local copies, waits for them, and re-layouts  1.38 us (1%)
    pallas_call x1, Pallas kernels, local(): pl.pallas_call(kernel, out_shape=jax.ShapeDtypeStruct(density.shape, f32)...  111 us

profile of v11, /device:TPU:1, one launch (start us, length us, event | category | flops | bytes accessed | tf_op | source)
XLA Modules:
  0.0 112.1 jit_solution(18255286581937347494)
XLA Ops:
  0.0 0.0 copy-start
  0.0 0.7 copy-done
  0.7 110.7 %shard_map.28 = f32[256,256]{1,0:T(8,128)S(1)} custom-call(s32[2,2]{1,0:T(2,128)S(1)} %copy-done, f32[256,256]{1,0:T(8,128)} %density.1), custom_call_target="tpu_custom_call" | custom-call | tf_op jit(solution)/shard_map/pallas_call | solution.py:405
  111.4 0.7 copy.4
Async XLA Ops:
  0.0 0.7 copy-start

commit v12 on v11

--- a/solution.py
+++ b/solution.py
@@ -239,8 +239,10 @@
 
     sibling = (z * 2 + 1 - core, c)
 
+    mirror = 1 - 2 * core
+
     def k_row(dx, dy):
-        return ((y - dy + NY) % NY) * NX + (x - dx + NX) % NX
+        return ((y - dy * mirror + NY) % NY) * NX + (x - dx * mirror + NX) % NX
 
     def k_col(dz, other):
         return ((z - dz + NZ) % NZ) * 2 + (1 - core if other else core)
@@ -305,7 +307,7 @@
             src, dst = ref.at[held, here], ref.at[SLOTS.index(b), here]
         if where and p == 0 and held == 0 and (b == 0 or a == "g0"):
             src = density.at[pl.ds((2 * h + plan) * step_rows, step_rows)]
-        target = device(**{"d" + where[0]: where[1]}) if where else sibling
+        target = device(**{"d" + where[0]: where[1] * mirror}) if where else sibling
         return remote(src, dst, row_send.at[p], row_recv.at[ROW[piece]], target)
 
     def col_copy(piece, where):
@@ -352,7 +354,7 @@
             keys = GROUPS[name[1:]]
             if isinstance(keys[0][1], bool):
                 places = [k_col(*key) for key in keys]
-                steps = [((x - k % NX + NX) % NX, (y - k // NX + NY) % NY) for k in places]
+                steps = [(((x - k % NX) * mirror + NX) % NX, ((y - k // NX) * mirror + NY) % NY) for k in places]
             else:
                 places = [k_row(*key) for key in keys]
                 steps = [(dx % NX, dy % NY) for dx, dy in keys]

time: 112 us -> 112 us (level)
  no operation moved by 1% of the time
where the time goes in v12:
time: 112 us; the launch traced here: 111 us
  Pallas kernels  110 us (98%)
  local copies, waits for them, and re-layouts  1.38 us (1%)
    pallas_call x1, Pallas kernels, local(): pl.pallas_call(kernel, out_shape=jax.ShapeDtypeStruct(density.shape, f32)...  110 us

profile of v12, /device:TPU:1, one launch (start us, length us, event | category | flops | bytes accessed | tf_op | source)
XLA Modules:
  0.0 111.3 jit_solution(1349334216913235600)
XLA Ops:
  0.0 0.0 copy-start
  0.0 0.7 copy-done
  0.7 109.9 %shard_map.28 = f32[256,256]{1,0:T(8,128)S(1)} custom-call(s32[2,2]{1,0:T(2,128)S(1)} %copy-done, f32[256,256]{1,0:T(8,128)} %density.1), custom_call_target="tpu_custom_call" | custom-call | tf_op jit(solution)/shard_map/pallas_call | solution.py:407
  110.6 0.7 copy.4
Async XLA Ops:
  0.0 0.7 copy-start

commit v13 on v12

--- a/solution.py
+++ b/solution.py
@@ -25,9 +25,9 @@
 
 ROWS64, HOP, SMALL, DOT, DOT_TILE = 1.4, 2.2, 0.02, 0.1, 0.1
 NEAR_FIRST = [
-    [(0, 0), (1, 0), (-1, 0), (0, 1), (0, -1)],
-    [(2, 0), (0, 2), (1, 1), (1, -1), (-1, 1), (-1, -1)],
-    [(1, 2), (-1, 2), (2, 1), (2, -1)],
+    [(0, 0), (1, 0), (-1, 0)], [(0, 1), (0, -1)],
+    [(2, 0), (0, 2)], [(1, 1), (1, -1), (-1, 1), (-1, -1)],
+    [(1, 2), (-1, 2)], [(2, 1), (2, -1)],
     [(2, 2)],
 ]
 COL_GROUPS = [[0], [1, -1], [2, -2], [3, -3], [4]]
@@ -38,9 +38,9 @@
 STREAMS = [HALVES, SQUARE, HALVES, SQUARE, HALVES]
 COLUMNS = [(0, 128, 0, 128), (128, 128, 0, 128), (0, 128, 128, 128), (128, 128, 128, 128)]
 SLOTS = (0, 1, -1, 2)
-SETS = [((0, 1), (1, 2), (3, 1)), ((0, 1), (1, 3))]
+SETS = [((0, 1), (1, 1), (2, 1), (3, 1)), ((0, 1), (1, 3))]
 SET_CHOICE = [[0, 0], [0, 0, 0], [0, 0], [0, 0, 0]]
-FAR = [(0, 1, 0), (0, 1)]
+FAR = [(0, 1, 0, 1), (0, 1)]
 
 
 def sets_of(p, h):

time: 112 us -> 112 us (level)
  no operation moved by 1% of the time
where the time goes in v13:
time: 112 us; the launch traced here: 111 us
  Pallas kernels  110 us (98%)
  local copies, waits for them, and re-layouts  1.38 us (1%)
    pallas_call x1, Pallas kernels, local(): pl.pallas_call(kernel, out_shape=jax.ShapeDtypeStruct(density.shape, f32)...  110 us

profile of v13, /device:TPU:1, one launch (start us, length us, event | category | flops | bytes accessed | tf_op | source)
XLA Modules:
  0.0 111.4 jit_solution(12148100495348175111)
XLA Ops:
  0.0 0.0 copy-start
  0.0 0.7 copy-done
  0.7 110.0 %shard_map.28 = f32[256,256]{1,0:T(8,128)S(1)} custom-call(s32[2,2]{1,0:T(2,128)S(1)} %copy-done, f32[256,256]{1,0:T(8,128)} %density.1), custom_call_target="tpu_custom_call" | custom-call | tf_op jit(solution)/shard_map/pallas_call | solution.py:407
  110.7 0.7 copy.4
Async XLA Ops:
  0.0 0.7 copy-start

commit v14 on v12

--- a/solution.py
+++ b/solution.py
@@ -16,9 +16,10 @@
 RING = (0, 1, -1, 2, -2, 3, -3, 4)
 
 GROUPS = {}
-BEGIN_ROWS = [(0, "g1"), (1, "g1")]
+AFTER_RING = []
+BEGIN_ROWS = [(0, "g2"), (1, "g2")]
 COL_SIZE = 1.0
-BEGIN_COLS = {}
+BEGIN_COLS = {2: (1, 1), 3: (1, 2)}
 LATER_COLS = {}
 DIRECT = set()
 BEGIN = [(0, "g1"), (1, "g1")]
@@ -102,7 +103,7 @@
         jobs[name] = (priority, cost + SMALL * (len(pushes) + len(needs)), needs, list(pushes))
 
     add(("start",), 0, SMALL, [], own_row(0, 0) + own_col(0, [t for t in range(4) if t not in BEGIN_COLS]))
-    add(("begin", 0, 1), 0, 0, [("turn", 0, 0, *key) for key in BEGIN_ROWS], own_row(0, 1))
+    add(("begin", 0, 1), 0, 0, [("turn", 0, 0, *key) for key in BEGIN_ROWS] + [("ring", 0, t, dz) for t, dz in AFTER_RING], own_row(0, 1))
     for t, (behind, dz) in BEGIN_COLS.items():
         add(("begin_col", t), 0, 0, [("ring", 0, behind, sign * dz) for sign in (1, -1)], own_col(0, (t,)))
     for t, (behind, dz) in LATER_COLS.items():

time: 112 us -> 112 us (level)
  no operation moved by 1% of the time
where the time goes in v14:
time: 112 us
  Pallas kernels  110 us (98%)
  local copies, waits for them, and re-layouts  1.38 us (1%)
    pallas_call x1, Pallas kernels, local(): pl.pallas_call(kernel, out_shape=jax.ShapeDtypeStruct(density.shape, f32)...  110 us

profile of v14, /device:TPU:1, one launch (start us, length us, event | category | flops | bytes accessed | tf_op | source)
XLA Modules:
  0.0 111.7 jit_solution(11135543213134399192)
XLA Ops:
  0.0 0.0 copy-start
  0.0 0.7 copy-done
  0.7 110.3 %shard_map.28 = f32[256,256]{1,0:T(8,128)S(1)} custom-call(s32[2,2]{1,0:T(2,128)S(1)} %copy-done, f32[256,256]{1,0:T(8,128)} %density.1), custom_call_target="tpu_custom_call" | custom-call | tf_op jit(solution)/shard_map/pallas_call | solution.py:408
  111.0 0.7 copy.4
Async XLA Ops:
  0.0 0.7 copy-start

commit v15 on v12

--- a/solution.py
+++ b/solution.py
@@ -17,7 +17,6 @@
 
 GROUPS = {}
 BEGIN_ROWS = [(0, "g1"), (1, "g1")]
-COL_SIZE = 1.0
 BEGIN_COLS = {}
 LATER_COLS = {}
 DIRECT = set()
@@ -36,7 +35,7 @@
 HALVES = [(0, 128, 0, 256), (128, 128, 0, 256)]
 SQUARE = [(0, 128, 0, 128), (0, 128, 128, 128), (128, 128, 0, 256)]
 STREAMS = [HALVES, SQUARE, HALVES, SQUARE, HALVES]
-COLUMNS = [(0, 128, 0, 128), (128, 128, 0, 128), (0, 128, 128, 128), (128, 128, 128, 128)]
+COLUMNS = [(0, 128, 0, 128), (128, 64, 0, 128), (192, 64, 0, 128), (0, 128, 128, 128), (128, 64, 128, 128), (192, 64, 128, 128)]
 SLOTS = (0, 1, -1, 2)
 SETS = [((0, 1), (1, 2), (3, 1)), ((0, 1), (1, 3))]
 SET_CHOICE = [[0, 0], [0, 0, 0], [0, 0], [0, 0, 0]]
@@ -89,10 +88,13 @@
                     pushes.append((link(plan, axis, sign), row_size(p, h), ("row", p, h, plan, a, b)))
         return pushes
 
+    def col_size(t):
+        return COLUMNS[t][1] * COLUMNS[t][3] / (64 * 256)
+
     def own_col(s, ts):
         pushes = []
         for t in ts:
-            pushes += [(("z", step), COL_SIZE, ("col", s, t, step, "h")) for step in ((1, -1, 2, -2) if (s, t) in DIRECT else (1, -1))]
+            pushes += [(("z", step), col_size(t), ("col", s, t, step, "h")) for step in ((1, -1, 2, -2) if (s, t) in DIRECT else (1, -1))]
         return pushes + [(("core", 0), 0.15, ("col", s, t, 0, "s")) for t in ts]
 
     def overlap(one, other):
@@ -101,7 +103,7 @@
     def add(name, priority, cost, needs, pushes=()):
         jobs[name] = (priority, cost + SMALL * (len(pushes) + len(needs)), needs, list(pushes))
 
-    add(("start",), 0, SMALL, [], own_row(0, 0) + own_col(0, [t for t in range(4) if t not in BEGIN_COLS]))
+    add(("start",), 0, SMALL, [], own_row(0, 0) + own_col(0, [t for t in range(len(COLUMNS)) if t not in BEGIN_COLS]))
     add(("begin", 0, 1), 0, 0, [("turn", 0, 0, *key) for key in BEGIN_ROWS], own_row(0, 1))
     for t, (behind, dz) in BEGIN_COLS.items():
         add(("begin_col", t), 0, 0, [("ring", 0, behind, sign * dz) for sign in (1, -1)], own_col(0, (t,)))
@@ -127,21 +129,21 @@
                     add(("pass", p, h, plan, "g%d" % g), 0, 0, [("row", p, h, plan, "g%d" % g, sign)],
                         [(link(plan, 1, sign), size * count, ("row", p, h, plan, "g%d" % g, 2))])
         if p % 2 == 0:
-            for t, dz in ((t, dz) for dz in RING for t in range(4)):
+            for t, dz in ((t, dz) for dz in RING for t in range(len(COLUMNS))):
                 pushes = []
                 if dz:
                     sign = 1 if dz > 0 else -1
                     if (s, t) in DIRECT:
                         if abs(dz) == 2:
-                            pushes.append((("z", sign), COL_SIZE, ("col", s, t, dz + sign, "h")))
-                            pushes.append((("z", 2 * sign), COL_SIZE / 2, ("col", s, t, 4, "q0" if sign == 1 else "q1")))
+                            pushes.append((("z", sign), col_size(t), ("col", s, t, dz + sign, "h")))
+                            pushes.append((("z", 2 * sign), col_size(t) / 2, ("col", s, t, 4, "q0" if sign == 1 else "q1")))
                     elif abs(dz) < 3:
-                        pushes.append((("z", sign), COL_SIZE, ("col", s, t, dz + sign, "h")))
+                        pushes.append((("z", sign), col_size(t), ("col", s, t, dz + sign, "h")))
                     elif dz != 4:
-                        pushes.append((("z", sign), COL_SIZE / 2, ("col", s, t, 4, "q0" if sign == 1 else "q1")))
+                        pushes.append((("z", sign), col_size(t) / 2, ("col", s, t, 4, "q0" if sign == 1 else "q1")))
                     pushes.append((("core", 0), 0.15, ("col", s, t, dz, "s")))
                     add(("ring", s, t, dz), 0, 0, col_tile(s, t, dz, False), pushes)
-                before = [("ring", s, t, dz)] if dz else [("start",) if p == 0 else ("final", p - 1, t % 2)]
+                before = [("ring", s, t, dz)] if dz else [("start",) if p == 0 else ("final", p - 1, COLUMNS[t][0] // 128)]
                 add(("split", s, t, dz, False), 2, SMALL, before)
                 add(("split", s, t, dz, True), 2, SMALL, col_tile(s, t, dz, True))
         for o, target in enumerate(STREAMS[p + 1]):
@@ -165,7 +167,7 @@
                 GROUPS[p, o, n] = group
             pushes = []
             if p < 2 * STEPS - 1:
-                pushes = own_row(p + 1, o) + (own_col(s + 1, [t for t in (o, 2 + o) if t not in LATER_COLS]) if p % 2 else [])
+                pushes = own_row(p + 1, o) + (own_col(s + 1, [t for t, col in enumerate(COLUMNS) if col[0] // 128 == o and t not in LATER_COLS]) if p % 2 else [])
             macs = [("mac", p, o, n) for n in range(len(groups))]
             if p % 2 == 0 and o == 2:
                 add(("final", p, o), 1, 2 * SMALL, macs)

time: 112 us -> 113 us (level)
  no operation moved by 1% of the time
where the time goes in v15:
time: 113 us; the launch traced here: 112 us
  Pallas kernels  111 us (98%)
  local copies, waits for them, and re-layouts  1.38 us (1%)
    pallas_call x1, Pallas kernels, local(): pl.pallas_call(kernel, out_shape=jax.ShapeDtypeStruct(density.shape, f32)...  111 us

profile of v15, /device:TPU:1, one launch (start us, length us, event | category | flops | bytes accessed | tf_op | source)
XLA Modules:
  0.0 112.2 jit_solution(17213745135655836726)
XLA Ops:
  0.0 0.0 copy-start
  0.0 0.7 copy-done
  0.7 110.8 %shard_map.28 = f32[256,256]{1,0:T(8,128)S(1)} custom-call(s32[2,2]{1,0:T(2,128)S(1)} %copy-done, f32[256,256]{1,0:T(8,128)} %density.1), custom_call_target="tpu_custom_call" | custom-call | tf_op jit(solution)/shard_map/pallas_call | solution.py:409
  111.5 0.7 copy.4
Async XLA Ops:
  0.0 0.7 copy-start

commit v16 on v15

--- a/solution.py
+++ b/solution.py
@@ -35,7 +35,7 @@
 HALVES = [(0, 128, 0, 256), (128, 128, 0, 256)]
 SQUARE = [(0, 128, 0, 128), (0, 128, 128, 128), (128, 128, 0, 256)]
 STREAMS = [HALVES, SQUARE, HALVES, SQUARE, HALVES]
-COLUMNS = [(0, 128, 0, 128), (128, 64, 0, 128), (192, 64, 0, 128), (0, 128, 128, 128), (128, 64, 128, 128), (192, 64, 128, 128)]
+COLUMNS = [(0, 128, 0, 256), (128, 128, 0, 128), (128, 128, 128, 128)]
 SLOTS = (0, 1, -1, 2)
 SETS = [((0, 1), (1, 2), (3, 1)), ((0, 1), (1, 3))]
 SET_CHOICE = [[0, 0], [0, 0, 0], [0, 0], [0, 0, 0]]

time: 113 us -> 112 us (level)
  no operation moved by 1% of the time
where the time goes in v16:
time: 112 us
  Pallas kernels  111 us (99%)
  local copies, waits for them, and re-layouts  1.38 us (1%)
    pallas_call x1, Pallas kernels, local(): pl.pallas_call(kernel, out_shape=jax.ShapeDtypeStruct(density.shape, f32)...  111 us

profile of v16, /device:TPU:1, one launch (start us, length us, event | category | flops | bytes accessed | tf_op | source)
XLA Modules:
  0.0 112.3 jit_solution(6639586499857186692)
XLA Ops:
  0.0 0.0 copy-start
  0.0 0.7 copy-done
  0.7 110.9 %shard_map.28 = f32[256,256]{1,0:T(8,128)S(1)} custom-call(s32[2,2]{1,0:T(2,128)S(1)} %copy-done, f32[256,256]{1,0:T(8,128)} %density.1), custom_call_target="tpu_custom_call" | custom-call | tf_op jit(solution)/shard_map/pallas_call | solution.py:409
  111.6 0.7 copy.4
Async XLA Ops:
  0.0 0.7 copy-start
